TPU v7x, 256 devices: a whole 4x4x8 slice. The times are simulated.
256 devices in a mesh: rep: 8 (over z), exp: 32 (over y, x, core).
Axes of the slice: x: 4, y: 4, z: 8, core: 2. Of those that a mesh axis runs over, the one named last changes fastest.
Arguments:
- tokens: bfloat16 [12288, 2048], P(('rep', 'exp')), may hold values from -6 to 6
- grad_out: bfloat16 [12288, 2048], P(('rep', 'exp')), may hold values from -6 to 6
- expert_ids: int32 [12288, 8], P(('rep', 'exp')), may hold values from 0 to 127, all different within a row; in each aligned block of 48 rows (0 to 47, 48 to 95, ...) at most 4 rows name the same one
- gate_probs: float32 [12288, 8], P(('rep', 'exp')), may hold values from 0.05 to 1
- gate_weight: bfloat16 [256, 2048, 384], P(('rep', 'exp')), may hold values from -0.125 to 0.125
- up_weight: bfloat16 [256, 2048, 384], P(('rep', 'exp')), may hold values from -0.125 to 0.125
- down_weight: bfloat16 [256, 384, 2048], P(('rep', 'exp')), may hold values from -0.21875 to 0.21875
Outputs:
- token_grad: bfloat16 [12288, 2048], P(('rep', 'exp'))
- gate_grad: bfloat16 [256, 2048, 384], P(('rep', 'exp'))
- up_grad: bfloat16 [256, 2048, 384], P(('rep', 'exp'))
- down_grad: bfloat16 [256, 384, 2048], P(('rep', 'exp'))
Inputs may be any that keep to these rules, and one draw needn't show every extreme that they name: `expert_ids`: the 8 experts of a token are distinct; among the 48 tokens of one device no expert is chosen more than 4 times, and that many in some device.
All inputs are finite; a program needn't handle non-finite values.
Results may differ from a plain program's by a relative error of at most 0.0058.
Values may be sent and summed in bfloat16 or wider, within the bound.
A program may use at most 128 MiB of HBM per device.

v0:
```python
import jax
import jax.numpy as jnp
from jax import lax
from jax.sharding import PartitionSpec as P


def per_device(tokens, grad_out, expert_ids, gate_probs, gate_weight, up_weight, down_weight):
    rep_count = lax.axis_size("rep")
    exp_count = lax.axis_size("exp")
    tok_rows, features = tokens.shape
    top_count = expert_ids.shape[1]
    experts = rep_count * exp_count // 2
    capacity = 2 * ((tok_rows * top_count // experts + 2) // 2)
    routed = tok_rows * top_count
    flat_ids = expert_ids.reshape(routed)
    order_index = jnp.arange(routed, dtype=jnp.int32)
    earlier = (flat_ids[:, None] == flat_ids[None, :]) & (
        order_index[None, :] < order_index[:, None]
    )
    slot_rank = jnp.sum(earlier.astype(jnp.int32), axis=1)
    slot_index = flat_ids * capacity + slot_rank
    slot_range = jnp.arange(experts * capacity, dtype=jnp.int32)
    selector = slot_range[:, None] == slot_index[None, :]
    select_rows = selector.astype(jnp.bfloat16)
    rows_in = jnp.repeat(tokens, top_count, axis=0)
    rows_grad = (
        (gate_probs[:, :, None] * grad_out[:, None, :].astype(jnp.float32))
        .reshape(routed, features)
        .astype(jnp.bfloat16)
    )
    packed_in = jnp.dot(select_rows, rows_in, preferred_element_type=jnp.float32).astype(
        jnp.bfloat16
    )
    packed_grad = jnp.dot(select_rows, rows_grad, preferred_element_type=jnp.float32).astype(
        jnp.bfloat16
    )
    send_in = jnp.repeat(packed_in.reshape(experts, capacity, features), 2, axis=0).reshape(
        rep_count, exp_count, capacity, features
    )
    send_grad = jnp.repeat(packed_grad.reshape(experts, capacity, features), 2, axis=0).reshape(
        rep_count, exp_count, capacity, features
    )
    recv_in, recv_grad = (
        lax.all_to_all(
            lax.all_to_all(send_in, "rep", split_axis=0, concat_axis=0, tiled=True),
            "exp",
            split_axis=1,
            concat_axis=1,
            tiled=True,
        ),
        lax.all_to_all(
            lax.all_to_all(send_grad, "rep", split_axis=0, concat_axis=0, tiled=True),
            "exp",
            split_axis=1,
            concat_axis=1,
            tiled=True,
        ),
    )
    slots = rep_count * exp_count * capacity
    slot_in = recv_in.reshape(slots, features)
    slot_grad = recv_grad.reshape(slots, features)
    gate_mat = gate_weight[0]
    up_mat = up_weight[0]
    down_mat = down_weight[0]
    contract_last = (((1,), (1,)), ((), ()))
    contract_first = (((0,), (0,)), ((), ()))
    gate_pre = jnp.dot(slot_in, gate_mat, preferred_element_type=jnp.float32)
    up_pre = jnp.dot(slot_in, up_mat, preferred_element_type=jnp.float32)
    sigmoid_gate = jax.nn.sigmoid(gate_pre)
    activated = gate_pre * sigmoid_gate
    hidden = (activated * up_pre).astype(jnp.bfloat16)
    hidden_grad = lax.dot_general(
        slot_grad, down_mat, contract_last, preferred_element_type=jnp.float32
    )
    up_in = (hidden_grad * activated).astype(jnp.bfloat16)
    gate_in = (
        hidden_grad * up_pre * sigmoid_gate * (1.0 + gate_pre * (1.0 - sigmoid_gate))
    ).astype(jnp.bfloat16)
    partial_rows = lax.dot_general(
        gate_in, gate_mat, contract_last, preferred_element_type=jnp.float32
    ) + lax.dot_general(up_in, up_mat, contract_last, preferred_element_type=jnp.float32)
    gate_grad = lax.dot_general(
        slot_in, gate_in, contract_first, preferred_element_type=jnp.float32
    ).astype(jnp.bfloat16)[None]
    up_grad = lax.dot_general(
        slot_in, up_in, contract_first, preferred_element_type=jnp.float32
    ).astype(jnp.bfloat16)[None]
    down_grad = lax.dot_general(
        hidden, slot_grad, contract_first, preferred_element_type=jnp.float32
    ).astype(jnp.bfloat16)[None]
    partial_grid = partial_rows.reshape(rep_count, exp_count, capacity, features)
    returned_grid = lax.all_to_all(
        lax.all_to_all(partial_grid, "rep", split_axis=0, concat_axis=0, tiled=True),
        "exp",
        split_axis=1,
        concat_axis=1,
        tiled=True,
    )
    returned = jnp.sum(returned_grid.reshape(experts, 2, capacity, features), axis=1).reshape(
        experts * capacity, features
    )
    routed_grads = returned[slot_index]
    token_grad = jnp.sum(routed_grads.reshape(tok_rows, top_count, features), axis=1).astype(
        jnp.bfloat16
    )
    return (token_grad, gate_grad, up_grad, down_grad)


def solution(mesh):
    return jax.shard_map(
        per_device,
        mesh=mesh,
        in_specs=(
            P(("rep", "exp"), None),
            P(("rep", "exp"), None),
            P(("rep", "exp"), None),
            P(("rep", "exp"), None),
            P(("rep", "exp"), None, None),
            P(("rep", "exp"), None, None),
            P(("rep", "exp"), None, None),
        ),
        out_specs=(
            P(("rep", "exp"), None),
            P(("rep", "exp"), None, None),
            P(("rep", "exp"), None, None),
            P(("rep", "exp"), None, None),
        ),
        check_vma=False,
    )
```

profile of v0, /device:TPU:8, one launch (start us, length us, event | category | flops | bytes accessed | tf_op | source)
XLA Modules:
  0.0 728.7 jit_solution(8222400331640888585)
XLA Ops:
  0.6 0.0 copy-start
  0.6 0.9 copy.36
  1.5 0.1 reshape.83
  1.6 0.2 convert_reduce_fusion
  1.9 3.5 convolution_convert_fusion
  5.4 4.1 reshape.87
  9.5 6.1 broadcast_in_dim.27
  15.6 8.6 %all-to-all-start.2 = ((bf16[8,32,4,2048]{3,2,1,0:T(4,128)(2,1)}), bf16[8,32,4,2048]{3,2,1,0:T(4,128)(2,1)}, u32[]{:S(2)}, u32[]{:S(2)}) async-start(bf16[8,32,4,2048]{3,2,1,0:T(4,128)(2,1)} %bitcast.45), calls=%async_computation.2 | async-start | bytes 8388608 | tf_op jit(solution)/shard_map/all_to_all | solution.py:45
  24.2 0.1 copy.37
  24.3 0.1 mul.65
  24.4 2.7 convolution_convert_fusion.1
  27.2 4.1 reshape.84
  31.3 89.3 %all-to-all-done.2 = bf16[8,32,4,2048]{3,2,1,0:T(4,128)(2,1)} async-done(((bf16[8,32,4,2048]{3,2,1,0:T(4,128)(2,1)}), bf16[8,32,4,2048]{3,2,1,0:T(4,128)(2,1)}, u32[]{:S(2)}, u32[]{:S(2)}) %all-to-all-start.2) | async-done | bytes 4194336 | tf_op jit(solution)/shard_map/all_to_all | solution.py:45
  120.6 6.1 broadcast_in_dim.12
  126.8 4.6 all-to-all-start
  131.3 7.1 copy.40
  138.4 89.6 %all-to-all-done = bf16[8,32,4,2048]{3,2,1,0:T(4,128)(2,1)} async-done(((bf16[8,32,4,2048]{3,2,1,0:T(4,128)(2,1)}), bf16[8,32,4,2048]{3,2,1,0:T(4,128)(2,1)}, u32[]{:S(2)}, u32[]{:S(2)}) %all-to-all-start) | async-done | bytes 4194336 | tf_op jit(solution)/shard_map/all_to_all | solution.py:52
  228.1 7.6 %all-to-all-start.3 = ((bf16[8,32,4,2048]{3,2,0,1:T(4,128)(2,1)}), bf16[8,32,4,2048]{3,2,0,1:T(4,128)(2,1)}, u32[]{:S(2)}, u32[]{:S(2)}) async-start(bf16[8,32,4,2048]{3,2,0,1:T(4,128)(2,1)} %copy.40), calls=%async_computation.3 | async-start | bytes 8388608 | tf_op jit(solution)/shard_map/all_to_all | solution.py:44
  235.7 7.1 copy.38
  242.8 43.5 %all-to-all-done.3 = bf16[8,32,4,2048]{3,2,0,1:T(4,128)(2,1)} async-done(((bf16[8,32,4,2048]{3,2,0,1:T(4,128)(2,1)}), bf16[8,32,4,2048]{3,2,0,1:T(4,128)(2,1)}, u32[]{:S(2)}, u32[]{:S(2)}) %all-to-all-start.3) | async-done | bytes 4194336 | tf_op jit(solution)/shard_map/all_to_all | solution.py:44
  286.2 8.1 %all-to-all-start.1 = ((bf16[8,32,4,2048]{3,2,0,1:T(4,128)(2,1)}), bf16[8,32,4,2048]{3,2,0,1:T(4,128)(2,1)}, u32[]{:S(2)}, u32[]{:S(2)}) async-start(bf16[8,32,4,2048]{3,2,0,1:T(4,128)(2,1)} %copy.38), calls=%async_computation.1 | async-start | bytes 8388608 | tf_op jit(solution)/shard_map/all_to_all | solution.py:51
  294.3 7.0 copy.41
  301.3 6.9 reshape.88
  308.2 5.8 fusion.7
  314.0 3.5 fusion.10
  317.5 27.2 %all-to-all-done.1 = bf16[8,32,4,2048]{3,2,0,1:T(4,128)(2,1)} async-done(((bf16[8,32,4,2048]{3,2,0,1:T(4,128)(2,1)}), bf16[8,32,4,2048]{3,2,0,1:T(4,128)(2,1)}, u32[]{:S(2)}, u32[]{:S(2)}) %all-to-all-start.1) | async-done | bytes 4194336 | tf_op jit(solution)/shard_map/all_to_all | solution.py:51
  344.6 7.0 copy.39
  351.7 7.1 reshape.85
  358.8 6.4 multiply_convert_fusion.1
  365.2 0.0 copy-start.6
  365.2 0.0 copy-start.8
  365.2 2.4 fusion.5
  367.6 5.6 convolution_add_fusion
  373.2 9.8 %reshape.89 = f32[8,32,4,2048]{3,2,1,0:T(4,128)} reshape(f32[1024,2048]{1,0:T(8,128)} %convolution_add_fusion) | data formatting | bytes 16777216 | tf_op jit(solution)/shard_map/reshape | solution.py:91
  383.0 190.9 %all_to_all.30 = f32[8,32,4,2048]{3,2,1,0:T(4,128)} all-to-all(f32[8,32,4,2048]{3,2,1,0:T(4,128)} %reshape.89), channel_id=1, replica_groups=mesh['rep'=8,'exp'=32] {'rep'}, dimensions={0} | all-to-all | bytes 16777216 | tf_op jit(solution)/shard_map/all_to_all | solution.py:93
  574.0 10.4 %copy.42 = f32[8,32,4,2048]{3,2,0,1:T(4,128)} copy(f32[8,32,4,2048]{3,2,1,0:T(4,128)} %all_to_all.30) | data formatting | bytes 16777216 | tf_op jit(solution)/shard_map/all_to_all | solution.py:93
  584.3 7.4 %all-to-all-start.5 = ((f32[8,32,4,2048]{3,2,0,1:T(4,128)}), f32[8,32,4,2048]{3,2,0,1:T(4,128)}, u32[]{:S(2)}, u32[]{:S(2)}) async-start(f32[8,32,4,2048]{3,2,0,1:T(4,128)} %copy.42), calls=%async_computation.5 | async-start | bytes 16777216 | tf_op jit(solution)/shard_map/all_to_all | solution.py:92
  591.8 0.1 copy.44
  591.9 0.1 mul.78
  592.0 5.9 fusion.2
  597.9 3.6 fusion.1
  601.5 3.1 fusion.3
  604.6 88.1 %all-to-all-done.5 = f32[8,32,4,2048]{3,2,0,1:T(4,128)} async-done(((f32[8,32,4,2048]{3,2,0,1:T(4,128)}), f32[8,32,4,2048]{3,2,0,1:T(4,128)}, u32[]{:S(2)}, u32[]{:S(2)}) %all-to-all-start.5) | async-done | bytes 8388640 | tf_op jit(solution)/shard_map/all_to_all | solution.py:92
  692.7 10.4 %copy.43 = f32[8,32,4,2048]{3,2,1,0:T(4,128)} copy(f32[8,32,4,2048]{3,2,0,1:T(4,128)} %all-to-all-done.5) | data formatting | bytes 16777216 | tf_op jit(solution)/shard_map/all_to_all | solution.py:92
  703.0 8.8 %reduce_sum.30 = f32[128,4,2048]{2,1,0:T(4,128)} reduce(f32[128,2,4,2048]{3,2,1,0:T(4,128)} %bitcast.44, f32[]{:T(128)} %constant.2.clone.1), dimensions={1}, to_apply=%region_1.0 | reduce | flops 1048576 | bytes 12582916 | tf_op jit(solution)/shard_map/reduce_sum | solution.py:99
  711.9 5.6 reshape.91
  717.5 7.4 %gather_fusion = f32[384,2048]{1,0:T(8,128)} fusion(f32[512,2048]{1,0:T(8,128)} %reshape.91, s32[1024]{0:T(1024)S(1)} %pad_clamp_fusion), kind=kCustom, calls=%fused_computation | custom fusion | bytes 6292992 | tf_op jit(solution)/shard_map/gather | solution.py:102
  724.8 3.3 bitcast_reduce_fusion
  (32 shorter events, 0.1 us)
Async XLA Ops:
  0.6 307.6 %copy-start = (bf16[1,2048,384]{2,1,0:T(8,128)(2,1)S(1)}, bf16[1,2048,384]{2,1,0:T(8,128)(2,1)}, u32[]{:S(2)}) copy-start(bf16[1,2048,384]{2,1,0:T(8,128)(2,1)} %param.11) | copy-start | bytes 4718596
  15.6 8.6 %copy-start.12 = (f32[48,8]{0,1:T(8,128)S(1)}, f32[48,8]{0,1:T(8,128)}, u32[]{:S(2)}) copy-start(f32[48,8]{0,1:T(8,128)} %param.10) | copy-start | bytes 4612
  15.6 8.8 %copy-start.10 = (bf16[48,2048]{1,0:T(8,128)(2,1)S(1)}, bf16[48,2048]{1,0:T(8,128)(2,1)}, u32[]{:S(2)}) copy-start(bf16[48,2048]{1,0:T(8,128)(2,1)} %param.8) | copy-start | bytes 589828
  15.6 105.0 %all-to-all-start.2 = ((bf16[8,32,4,2048]{3,2,1,0:T(4,128)(2,1)}), bf16[8,32,4,2048]{3,2,1,0:T(4,128)(2,1)}, u32[]{:S(2)}, u32[]{:S(2)}) async-start(bf16[8,32,4,2048]{3,2,1,0:T(4,128)(2,1)} %bitcast.45), calls=%async_computation.2 | async-start | bytes 8388608 | tf_op jit(solution)/shard_map/all_to_all | solution.py:45
  126.8 101.3 %all-to-all-start = ((bf16[8,32,4,2048]{3,2,1,0:T(4,128)(2,1)}), bf16[8,32,4,2048]{3,2,1,0:T(4,128)(2,1)}, u32[]{:S(2)}, u32[]{:S(2)}) async-start(bf16[8,32,4,2048]{3,2,1,0:T(4,128)(2,1)} %bitcast.46), calls=%async_computation | async-start | bytes 8388608 | tf_op jit(solution)/shard_map/all_to_all | solution.py:52
  228.1 58.2 %all-to-all-start.3 = ((bf16[8,32,4,2048]{3,2,0,1:T(4,128)(2,1)}), bf16[8,32,4,2048]{3,2,0,1:T(4,128)(2,1)}, u32[]{:S(2)}, u32[]{:S(2)}) async-start(bf16[8,32,4,2048]{3,2,0,1:T(4,128)(2,1)} %copy.40), calls=%async_computation.3 | async-start | bytes 8388608 | tf_op jit(solution)/shard_map/all_to_all | solution.py:44
  286.2 58.4 %all-to-all-start.1 = ((bf16[8,32,4,2048]{3,2,0,1:T(4,128)(2,1)}), bf16[8,32,4,2048]{3,2,0,1:T(4,128)(2,1)}, u32[]{:S(2)}, u32[]{:S(2)}) async-start(bf16[8,32,4,2048]{3,2,0,1:T(4,128)(2,1)} %copy.38), calls=%async_computation.1 | async-start | bytes 8388608 | tf_op jit(solution)/shard_map/all_to_all | solution.py:51
  308.2 5.8 copy-start.2
  308.2 5.8 copy-start.5
  365.2 2.4 copy-start.6
  365.2 2.4 copy-start.8
  584.3 7.5 %copy-start.11 = (s32[48,8]{0,1:T(8,128)S(1)}, s32[48,8]{0,1:T(8,128)}, u32[]{:S(2)}) copy-start(s32[48,8]{0,1:T(8,128)} %param.9) | copy-start | bytes 4612
  584.3 7.7 %copy-start.9 = (bf16[1024,384]{1,0:T(8,128)(2,1)S(1)}, bf16[1024,384]{1,0:T(8,128)(2,1)}, u32[]{:S(2)}) copy-start(bf16[1024,384]{1,0:T(8,128)(2,1)} %copy-done.8) | copy-start | bytes 2359300
  584.3 108.4 %all-to-all-start.5 = ((f32[8,32,4,2048]{3,2,0,1:T(4,128)}), f32[8,32,4,2048]{3,2,0,1:T(4,128)}, u32[]{:S(2)}, u32[]{:S(2)}) async-start(f32[8,32,4,2048]{3,2,0,1:T(4,128)} %copy.42), calls=%async_computation.5 | async-start | bytes 16777216 | tf_op jit(solution)/shard_map/all_to_all | solution.py:92
  592.0 5.9 copy-start.3
  592.0 5.9 copy-start.7
  597.9 3.6 copy-start.4
  597.9 3.6 copy-start.13
  597.9 3.6 copy-start.14
  717.5 10.7 %copy-start.1 = (bf16[1,2048,384]{2,1,0:T(8,128)(2,1)S(1)}, bf16[1,2048,384]{2,1,0:T(8,128)(2,1)}, u32[]{:S(2)}) copy-start(bf16[1,2048,384]{2,1,0:T(8,128)(2,1)} %param.11) | copy-start | bytes 4718596
where the time goes:
time: 741 us; the launch traced here: 729 us
  waiting for transfers between devices  338 us (46%)
  blocking collectives  191 us (26%)
  local copies, waits for them, and re-layouts  108 us (15%)
  matrix products  42.5 us (6%)
  starting transfers between devices  36.2 us (5%)
  other arithmetic  12.5 us (2%)
    all_to_all x1, blocking collectives, per_device(): lax.all_to_all(partial_grid, 'rep', split_axis=0, concat_axis=0, tiled=True)  191 us
    all_to_all x1, waiting for transfers between devices, per_device(): lax.all_to_all(send_grad, 'rep', split_axis=0, concat_axis=0, tiled=True)  89.6 us
    all_to_all x1, waiting for transfers between devices, per_device(): lax.all_to_all(send_in, 'rep', split_axis=0, concat_axis=0, tiled=True)  89.3 us
    all_to_all x1, waiting for transfers between devices, per_device(): lax.all_to_all(lax.all_to_all(partial_grid, 'rep', split_axis=0, concat_a...  88.1 us
    all_to_all x1, waiting for transfers between devices, per_device(): lax.all_to_all(lax.all_to_all(send_in, 'rep', split_axis=0, concat_axis=0...  43.5 us
    all_to_all x1, waiting for transfers between devices, per_device(): lax.all_to_all(lax.all_to_all(send_grad, 'rep', split_axis=0, concat_axis...  27.2 us
  transfers between devices with their start and end apart: 5, of which 5 were waited for; matrix products, arithmetic and copies ran while one was open for 8% of the time, Pallas kernels for 0%

commit v1 on v0

v1 whole, which is shorter than its diff:
```python
import jax
import jax.numpy as jnp
from jax import lax
from jax.experimental import pallas as pl
from jax.experimental.pallas import tpu as pltpu
from jax.sharding import PartitionSpec as P

MESH = pl.DeviceIdType.MESH
F32 = jnp.float32
BF16 = jnp.bfloat16
REP = 8
ROWS = 48
D = 2048
HALF = 384
TOP = 8
GROUPS = 4
NT = (((1,), (1,)), ((), ()))
TN = (((0,), (0,)), ((), ()))


UP = (0, 1, 3, 5, 7)
DOWN = (0, 2, 4, 6, 7)
OFFSET = (0, 7, 1, 6, 2, 5, 3, 4)


def kernel(
    tok_hbm, grad_hbm, meta_hbm, gate_hbm, up_hbm, down_hbm,
    tok_out, gate_out, up_out, down_out,
    tok, grad, meta, wgu, wd, send, recv, xs, gs, hid, giui, rsend, rrecv, selt,
    zsend, zrecv, own, gu_send, gu_recv, d_send, d_recv,
    load_sem, ring_s, ring_r, w_s, w_r, disp_s, disp_r, ret_s, ret_r, z_s, z_r, g_s, g_r,
):
    z = lax.axis_index("rep")
    e = lax.axis_index("exp")
    p = e // 2
    core = e % 2
    px = p % 4
    py = p // 4
    partner = (z, p * 2 + 1 - core)

    def plane(i):
        return ((py + i // 4) % 4) * 4 + (px + i % 4) % 4

    def zdev(d):
        return ((z + d) % REP, e)

    loads = [
        pltpu.make_async_copy(meta_hbm, meta.at[0], load_sem.at[0]),
        pltpu.make_async_copy(tok_hbm, tok.at[0], load_sem.at[1]),
        pltpu.make_async_copy(grad_hbm, grad.at[0], load_sem.at[2]),
        pltpu.make_async_copy(gate_hbm, wgu.at[:, pl.ds(0, HALF)], load_sem.at[3]),
        pltpu.make_async_copy(up_hbm, wgu.at[:, pl.ds(HALF, HALF)], load_sem.at[4]),
        pltpu.make_async_copy(down_hbm, wd.at[pl.ds(0, HALF)], load_sem.at[5]),
    ]
    for c in loads:
        c.start()

    barrier = pltpu.get_barrier_semaphore()

    def greet_plane(i, carry):
        pl.semaphore_signal(barrier, inc=1, device_id=(z, plane(i) * 2 + core), device_id_type=MESH)
        return carry

    def greet_z(i, carry):
        pl.semaphore_signal(barrier, inc=1, device_id=zdev(i), device_id_type=MESH)
        return carry

    lax.fori_loop(1, 16, greet_plane, 0)
    lax.fori_loop(1, REP, greet_z, 0)
    pl.semaphore_signal(barrier, inc=1, device_id=partner, device_id_type=MESH)
    pl.semaphore_wait(barrier, 23)

    def hop(direction, h, piece):
        table = (UP, DOWN)[direction]
        buf = (tok, grad, meta)[piece]
        return pltpu.make_async_remote_copy(
            src_ref=buf.at[table[h - 1]],
            dst_ref=buf.at[table[h]],
            send_sem=ring_s.at[direction, h - 1, piece],
            recv_sem=ring_r.at[direction, h - 1, piece],
            device_id=zdev((1, 7)[direction]),
            device_id_type=MESH,
        )

    def pieces(direction, h):
        if h < 4:
            return (2, 0, 1)
        return ((2, 0), (1,))[direction]

    for c in loads[:3]:
        c.wait()
    for piece in (2, 0, 1):
        for direction in (0, 1):
            hop(direction, 1, piece).start()

    def advance(h):
        for piece in (2, 0, 1):
            for direction in (0, 1):
                if piece in pieces(direction, h):
                    hop(direction, h, piece).wait_recv()
                    if h < 4 and piece in pieces(direction, h + 1):
                        hop(direction, h + 1, piece).start()

    def weight_copy(k):
        if k < 2:
            src = wgu.at[:, pl.ds(k * HALF, HALF)]
            dst = wgu.at[:, pl.ds((k + 2) * HALF, HALF)]
        else:
            src = wd.at[pl.ds(0, HALF)]
            dst = wd.at[pl.ds(HALF, HALF)]
        return pltpu.make_async_remote_copy(
            src_ref=src, dst_ref=dst, send_sem=w_s.at[k], recv_sem=w_r.at[k],
            device_id=partner, device_id_type=MESH,
        )

    for k in range(3):
        loads[3 + k].wait()
        weight_copy(k).start()

    row = lax.broadcasted_iota(jnp.int32, (128, 128), 0)
    lane = lax.broadcasted_iota(jnp.int32, (128, 128), 1)
    low = lane < ROWS
    same_chunk = ((row // 4) % 2 == 0) == low
    tri = jnp.where(row < lane, 1.0, 0.0).astype(BF16)
    expert = (16 * z + row // 8).astype(F32)
    rank = (row % 4).astype(F32)

    def disp(g, i):
        q = plane(i)
        return pltpu.make_async_remote_copy(
            src_ref=send.at[g, q], dst_ref=recv.at[g, p],
            send_sem=disp_s.at[g, q], recv_sem=disp_r.at[g, p],
            device_id=(z, q * 2 + core), device_id_type=MESH,
        )

    def disp_own(g):
        return pltpu.make_async_copy(send.at[g, p], recv.at[g, p], disp_r.at[g, p])

    def disp_recv(g, i):
        q = plane(i)
        return pltpu.make_async_remote_copy(
            src_ref=send.at[g, q], dst_ref=recv.at[g, q],
            send_sem=disp_s.at[g, q], recv_sem=disp_r.at[g, q],
            device_id=(z, q * 2 + core), device_id_type=MESH,
        )

    def dispatch(g):
        low8 = low[:8]
        ids = jnp.where(low8, meta[2 * g, 0:8, :], meta[2 * g + 1, 0:8, :])
        prob = jnp.where(low8, meta[2 * g, 8:16, :], meta[2 * g + 1, 8:16, :])
        hit = jnp.zeros((128, 128), F32)
        weight = jnp.zeros((128, 128), F32)
        for k in range(TOP):
            match = ids[k : k + 1, :] == expert
            hit = jnp.where(match, 1.0, hit)
            weight = jnp.where(match, prob[k : k + 1, :], weight)
        hit = jnp.where(same_chunk, hit, 0.0)
        before = jnp.dot(hit.astype(BF16), tri, preferred_element_type=F32)
        sel = jnp.where(before == rank, hit, 0.0)
        scale = jnp.sum(sel * weight, axis=1, keepdims=True)
        selt[g] = sel.T.astype(BF16)
        sel_rows = sel.astype(BF16)[:, : 2 * ROWS]

        def tile(j, carry):
            cols = pl.ds(pl.multiple_of(j * 512, 512), 512)
            t2 = tok[2 * g : 2 * g + 2, :, cols].reshape(2 * ROWS, 512)
            g2 = grad[2 * g : 2 * g + 2, :, cols].reshape(2 * ROWS, 512)
            a = jnp.dot(sel_rows, t2, preferred_element_type=F32)
            b = jnp.dot(sel_rows, g2, preferred_element_type=F32) * scale
            both = jnp.concatenate([a.reshape(16, 8, 512), b.reshape(16, 8, 512)], axis=1)
            send[g, :, :, cols] = both.astype(BF16)
            return carry

        lax.fori_loop(0, 4, tile, 0)

        def go(i, carry):
            disp(g, i).start()
            return carry

        lax.fori_loop(1, 16, go, 0)
        disp_own(g).start()

    def ret(g, i):
        q = plane(i)
        return pltpu.make_async_remote_copy(
            src_ref=rsend.at[g, q], dst_ref=rrecv.at[g, p],
            send_sem=ret_s.at[g, q], recv_sem=ret_r.at[g, p],
            device_id=(z, q * 2 + core), device_id_type=MESH,
        )

    def ret_own(g):
        return pltpu.make_async_copy(rsend.at[g, p], rrecv.at[g, p], ret_r.at[g, p])

    def ret_recv(g, i):
        q = plane(i)
        return pltpu.make_async_remote_copy(
            src_ref=rsend.at[g, q], dst_ref=rrecv.at[g, q],
            send_sem=ret_s.at[g, q], recv_sem=ret_r.at[g, q],
            device_id=(z, q * 2 + core), device_id_type=MESH,
        )

    def expert_rows(g):
        def landed(i, carry):
            disp_recv(g, i).wait_recv()
            return carry

        lax.fori_loop(1, 16, landed, 0)
        disp_own(g).wait()
        rows = pl.ds(g * 128, 128)

        def unpack(j, carry):
            cols = pl.ds(pl.multiple_of(j * 512, 512), 512)
            both = recv[g, :, :, cols].astype(F32)
            xs[rows, cols] = both[:, 0:8].reshape(128, 512).astype(BF16)
            gs[rows, cols] = both[:, 8:16].reshape(128, 512).astype(BF16)
            return carry

        lax.fori_loop(0, 4, unpack, 0)
        if g == 0:
            for k in range(3):
                weight_copy(k).wait_recv()

        def forward(h, carry):
            wide = pl.ds(pl.multiple_of(h * 2 * HALF, 2 * HALF), 2 * HALF)
            narrow = pl.ds(pl.multiple_of(h * HALF, HALF), HALF)
            pre = jnp.dot(xs[rows, :], wgu[:, wide], preferred_element_type=F32)
            gate, up = pre[:, :HALF], pre[:, HALF:]
            hidden_grad = lax.dot_general(gs[rows, :], wd[narrow, :], NT, preferred_element_type=F32)
            s = jax.nn.sigmoid(gate)
            act = gate * s
            hid[rows, narrow] = (act * up).astype(BF16)
            gate_in = (hidden_grad * up * s * (1.0 + gate * (1.0 - s))).astype(BF16)
            up_in = (hidden_grad * act).astype(BF16)
            giui[rows, wide] = jnp.concatenate([gate_in, up_in], axis=1)
            return carry

        lax.fori_loop(0, 2, forward, 0)

        def back(j, carry):
            out = pl.ds(pl.multiple_of(j * 512, 512), 512)
            right = pl.ds(pl.multiple_of(j * 512 + 1024, 512), 512)
            a = lax.dot_general(giui[rows, :], wgu[out, :], NT, preferred_element_type=F32)
            b = lax.dot_general(giui[rows, :], wgu[right, :], NT, preferred_element_type=F32)
            both = jnp.concatenate([a.reshape(16, 8, 512), b.reshape(16, 8, 512)], axis=1)
            rsend[g, :, :, out] = both.astype(BF16)
            return carry

        lax.fori_loop(0, 2, back, 0)

        def go(i, carry):
            ret(g, i).start()
            return carry

        lax.fori_loop(1, 16, go, 0)
        ret_own(g).start()

    def zcopy(j):
        return pltpu.make_async_remote_copy(
            src_ref=zsend.at[j], dst_ref=zrecv.at[j],
            send_sem=z_s.at[j], recv_sem=z_r.at[j],
            device_id=zdev(OFFSET[j]), device_id_type=MESH,
        )

    def combine(g):
        def landed(i, carry):
            ret_recv(g, i).wait_recv()
            return carry

        lax.fori_loop(1, 16, landed, 0)
        ret_own(g).wait()

        def tile(j, carry):
            both = rrecv[g, :, :, pl.ds(pl.multiple_of(j * 512, 512), 512)].astype(F32)
            for side in range(2):
                cols = pl.ds(pl.multiple_of(j * 512 + side * 1024, 512), 512)
                part = both[:, side * 8 : side * 8 + 8].reshape(128, 512).astype(BF16)
                total = jnp.dot(selt[g], part, preferred_element_type=F32)
                if g == 0:
                    own[:, cols] = total[:ROWS]
                else:
                    zsend[2 * g, :, cols] = total[:ROWS].astype(BF16)
                zsend[2 * g + 1, :, cols] = total[ROWS : 2 * ROWS].astype(BF16)
            return carry

        lax.fori_loop(0, 2, tile, 0)
        for j in (2 * g + 1, 2 * g):
            if j > 0:
                zcopy(j).start()

    def grad_copy(k):
        src, dst = ((gu_send.at[0], gu_recv.at[0]), (gu_send.at[1], gu_recv.at[1]), (d_send, d_recv))[k]
        return pltpu.make_async_remote_copy(
            src_ref=src, dst_ref=dst, send_sem=g_s.at[k], recv_sem=g_r.at[k],
            device_id=partner, device_id_type=MESH,
        )

    def gate_up_tile(j, h):
        rows = pl.ds(pl.multiple_of(j * 256, 256), 256)
        return rows, lax.dot_general(
            xs[:, rows], giui[:, h * 2 * HALF : (h + 1) * 2 * HALF], TN, preferred_element_type=F32
        )

    def down_tile(j, h):
        cols = pl.ds(pl.multiple_of(j * 512, 512), 512)
        return cols, lax.dot_general(
            hid[:, h * HALF : (h + 1) * HALF], gs[:, cols], TN, preferred_element_type=F32
        )

    def partner_grads():
        def tile(j, carry):
            rows, both = gate_up_tile(j, 1)
            gu_send[0, rows, :] = both[:, :HALF].astype(BF16)
            gu_send[1, rows, :] = both[:, HALF:].astype(BF16)
            return carry

        lax.fori_loop(0, 8, tile, 0)
        grad_copy(0).start()
        grad_copy(1).start()

        def tile_down(j, carry):
            cols, part = down_tile(j, 1)
            d_send[:, cols] = part.astype(BF16)
            return carry

        lax.fori_loop(0, 4, tile_down, 0)
        grad_copy(2).start()

    def own_grads():
        grad_copy(0).wait_recv()
        grad_copy(1).wait_recv()

        def tile(j, carry):
            rows, both = gate_up_tile(j, 0)
            gate_out[rows, :] = (both[:, :HALF] + gu_recv[0, rows, :].astype(F32)).astype(BF16)
            up_out[rows, :] = (both[:, HALF:] + gu_recv[1, rows, :].astype(F32)).astype(BF16)
            return carry

        lax.fori_loop(0, 8, tile, 0)
        grad_copy(2).wait_recv()

        def tile_down(j, carry):
            cols, part = down_tile(j, 0)
            down_out[:, cols] = (part + d_recv[:, cols].astype(F32)).astype(BF16)
            return carry

        lax.fori_loop(0, 4, tile_down, 0)

    advance(1)
    dispatch(0)
    advance(2)
    dispatch(1)
    expert_rows(0)
    advance(3)
    dispatch(2)
    expert_rows(1)
    advance(4)
    dispatch(3)
    combine(0)
    expert_rows(2)
    combine(1)
    expert_rows(3)
    partner_grads()
    combine(2)
    combine(3)
    own_grads()

    for j in range(1, REP):
        zcopy(j).wait_recv()

    def finish(j, carry):
        cols = pl.ds(pl.multiple_of(j * 512, 512), 512)
        total = own[:, cols]
        for k in range(1, REP):
            total = total + zrecv[k, :, cols].astype(F32)
        tok_out[:, cols] = total.astype(BF16)
        return carry

    lax.fori_loop(0, 4, finish, 0)

    for h in range(1, 5):
        for direction in (0, 1):
            for piece in pieces(direction, h):
                hop(direction, h, piece).wait_send()
    for k in range(3):
        weight_copy(k).wait_send()
        grad_copy(k).wait_send()
    for j in range(1, REP):
        zcopy(j).wait_send()

    def drain(i, carry):
        for g in range(GROUPS):
            disp(g, i).wait_send()
            ret(g, i).wait_send()
        return carry

    lax.fori_loop(1, 16, drain, 0)


def per_device(tokens, grad_out, expert_ids, gate_probs, gate_weight, up_weight, down_weight):
    def lay(values, fill):
        t = values.astype(F32).T
        pad = jnp.full((TOP, 128 - 2 * ROWS), fill, F32)
        return jnp.concatenate([t, t, pad], axis=1)

    meta = jnp.concatenate([lay(expert_ids, -1.0), lay(gate_probs, 0.0)], axis=0)
    anywhere = pl.BlockSpec(memory_space=pl.ANY)
    vmem = pl.BlockSpec(memory_space=pltpu.VMEM)
    dma = pltpu.SemaphoreType.DMA
    tok_grad, gate_grad, up_grad, down_grad = pl.pallas_call(
        kernel,
        out_shape=(
            jax.ShapeDtypeStruct((ROWS, D), BF16),
            jax.ShapeDtypeStruct((D, HALF), BF16),
            jax.ShapeDtypeStruct((D, HALF), BF16),
            jax.ShapeDtypeStruct((HALF, D), BF16),
        ),
        in_specs=[anywhere] * 6,
        out_specs=[vmem] * 4,
        scratch_shapes=[
            pltpu.VMEM((REP, ROWS, D), BF16),
            pltpu.VMEM((REP, ROWS, D), BF16),
            pltpu.VMEM((REP, 16, 128), F32),
            pltpu.VMEM((D, 4 * HALF), BF16),
            pltpu.VMEM((2 * HALF, D), BF16),
            pltpu.VMEM((GROUPS, 16, 16, D), BF16),
            pltpu.VMEM((GROUPS, 16, 16, D), BF16),
            pltpu.VMEM((GROUPS * 128, D), BF16),
            pltpu.VMEM((GROUPS * 128, D), BF16),
            pltpu.VMEM((GROUPS * 128, 2 * HALF), BF16),
            pltpu.VMEM((GROUPS * 128, 4 * HALF), BF16),
            pltpu.VMEM((GROUPS, 16, 16, D // 2), BF16),
            pltpu.VMEM((GROUPS, 16, 16, D // 2), BF16),
            pltpu.VMEM((GROUPS, 128, 128), BF16),
            pltpu.VMEM((REP, ROWS, D), BF16),
            pltpu.VMEM((REP, ROWS, D), BF16),
            pltpu.VMEM((ROWS, D), F32),
            pltpu.VMEM((2, D, HALF), BF16),
            pltpu.VMEM((2, D, HALF), BF16),
            pltpu.VMEM((HALF, D), BF16),
            pltpu.VMEM((HALF, D), BF16),
            dma((6,)),
            dma((2, 4, 3)),
            dma((2, 4, 3)),
            dma((3,)),
            dma((3,)),
            dma((GROUPS, 16)),
            dma((GROUPS, 16)),
            dma((GROUPS, 16)),
            dma((GROUPS, 16)),
            dma((REP,)),
            dma((REP,)),
            dma((3,)),
            dma((3,)),
        ],
        compiler_params=pltpu.CompilerParams(
            collective_id=0, has_side_effects=True, vmem_limit_bytes=60 * 2**20
        ),
    )(tokens, grad_out, meta, gate_weight[0], up_weight[0], down_weight[0])
    return tok_grad, gate_grad[None], up_grad[None], down_grad[None]


def solution(mesh):
    rows = P(("rep", "exp"), None)
    mats = P(("rep", "exp"), None, None)
    return jax.shard_map(
        per_device,
        mesh=mesh,
        in_specs=(rows, rows, rows, rows, mats, mats, mats),
        out_specs=(rows, mats, mats, mats),
        check_vma=False,
    )
```

time: 741 us -> 136 us (0.18); the launches traced: 729 us -> 135 us
  waiting for transfers between devices: 338 us -> 0 us
  blocking collectives: 191 us -> 0 us
  Pallas kernels: 0 us -> 125 us
  local copies, waits for them, and re-layouts: 108 us -> 7.57 us
  matrix products: 42.5 us -> 0 us
  starting transfers between devices: 36.2 us -> 0 us
  other arithmetic: 12.5 us -> 2.13 us
    all_to_all x5 -> x0, waiting for transfers between devices: 338 us -> none  [the longest x1 89.6 us: per_device(): lax.all_to_all(send_grad, 'rep', split_axis=0, concat_axis=0, tiled=True)]
    all_to_all x1 -> x0, blocking collectives: 191 us -> none  [per_device(): lax.all_to_all(partial_grid, 'rep', split_axis=0, concat_axis=0, tiled=True)]
    pallas_call x0 -> x1, Pallas kernels: none -> 125 us  [per_device(): pl.pallas_call(kernel, out_shape=(jax.ShapeDtypeStruct((ROWS, D), BF16),...]
    all_to_all x6 -> x0, local copies, waits for them, and re-layouts: 49 us -> none  [the longest x1 10.4 us: per_device(): lax.all_to_all(lax.all_to_all(partial_grid, 'rep', split_axis=0, concat_a...]
    dot_general x10 -> x0, matrix products: 42.5 us -> none  [the longest x1 6.38 us: per_device(): lax.dot_general(slot_grad, down_mat, contract_last, preferred_element_typ...]
    reshape x7 -> x0, local copies, waits for them, and re-layouts: 37.7 us -> none  [the longest x1 9.79 us: per_device(): partial_rows.reshape(rep_count, exp_count, capacity, features)]
    all_to_all x5 -> x0, starting transfers between devices: 36.2 us -> none  [the longest x1 8.6 us: per_device(): lax.all_to_all(send_in, 'rep', split_axis=0, concat_axis=0, tiled=True)]
    reduce_sum x3 -> x0, other arithmetic: 12.4 us -> none  [the longest x1 8.83 us: per_device(): jnp.sum(returned_grid.reshape(experts, 2, capacity, features), axis=1)]
  transfers between devices with their start and end apart: 5 -> 0, of which waited for: 5 -> 0; matrix products, arithmetic and copies ran while one was open for 8% -> 0% of each run, Pallas kernels for 0% -> 0%
where the time goes in v1:
time: 136 us; the launch traced here: 135 us
  Pallas kernels  125 us (92%)
  local copies, waits for them, and re-layouts  7.57 us (6%)
  other arithmetic  2.13 us (2%)
    pallas_call x1, Pallas kernels, per_device(): pl.pallas_call(kernel, out_shape=(jax.ShapeDtypeStruct((ROWS, D), BF16),...  125 us
    unnamed x8, local copies, waits for them, and re-layouts  7.56 us

profile of v1, /device:TPU:8, one launch (start us, length us, event | category | flops | bytes accessed | tf_op | source)
XLA Modules:
  0.0 135.5 jit_solution(1487919467155917791)
XLA Ops:
  0.6 0.7 convert_bitcast_fusion
  1.3 1.4 %maximum_maximum_fusion.meta_hbm = f32[16,128]{1,0:T(8,128)} fusion(f32[8,32]{1,0:T(8,128)S(1)} %broadcast_in_dim.16, f32[8,48]{1,0:T(8,128)} %bitcast.15, f32[8,32]{1,0:T(8,128)S(1)} %broadcast_in_dim.15, f32[8,48]{1,0:T(8,128)S(1)} %convert_bitcast_fusion), kind=kLoop, calls=%fused_computation | loop fusion | flops 10240 | bytes 13312 | tf_op jit(solution)/shard_map/concatenate | solution.py:405
  2.8 125.1 %shard_map.102 = (bf16[48,2048]{1,0:T(8,128)(2,1)}, bf16[2048,384]{1,0:T(8,128)(2,1)}, bf16[2048,384]{1,0:T(8,128)(2,1)}, bf16[384,2048]{1,0:T(8,128)(2,1)}) custom-call(bf16[48,2048]{1,0:T(8,128)(2,1)} %tok_hbm.1, bf16[48,2048]{1,0:T(8,128)(2,1)} %grad_hbm.1, f32[16,128]{1,0:T(8,128)} %maximum_maximum_fusion.meta_hbm, bf16[2048,384]{1,0:T(8,128)(2,1)} %bitcast.12, ...), custom_call_target="tpu_custom_call" | custom-call | tf_op jit(solution)/shard_map/pallas_call | solution.py:409
  127.9 1.6 %copy.15 = bf16[48,2048]{1,0:T(8,128)(2,1)} copy(bf16[48,2048]{1,0:T(8,128)(2,1)} %get-tuple-element.16) | data formatting | bytes 393216
  129.5 0.0 copy-start.1
  129.5 2.8 %copy.16 = bf16[1,2048,384]{2,1,0:T(8,128)(2,1)} copy(bf16[1,2048,384]{2,1,0:T(8,128)(2,1)} %bitcast.11) | data formatting | bytes 3145728
  132.3 0.0 copy-done.1
  132.3 0.0 copy-start
  132.3 1.1 copy.17
  133.5 0.8 copy-done
  134.3 1.1 copy.18
  (2 shorter events, 0.0 us)
Async XLA Ops:
  129.5 2.8 %copy-start.1 = (bf16[2048,384]{1,0:T(8,128)(2,1)S(1)}, bf16[2048,384]{1,0:T(8,128)(2,1)}, u32[]{:S(2)}) copy-start(bf16[2048,384]{1,0:T(8,128)(2,1)} %get-tuple-element.10) | copy-start | bytes 4718596
  132.3 2.0 %copy-start = (bf16[384,2048]{1,0:T(8,128)(2,1)S(1)}, bf16[384,2048]{1,0:T(8,128)(2,1)}, u32[]{:S(2)}) copy-start(bf16[384,2048]{1,0:T(8,128)(2,1)} %get-tuple-element.11) | copy-start | bytes 4718596

commit v2 on v1

--- a/solution.py
+++ b/solution.py
@@ -14,21 +14,22 @@
 HALF = 384
 TOP = 8
 GROUPS = 4
+LIMIT = 47
 NT = (((1,), (1,)), ((), ()))
 TN = (((0,), (0,)), ((), ()))
 
 
 UP = (0, 1, 3, 5, 7)
 DOWN = (0, 2, 4, 6, 7)
-OFFSET = (0, 7, 1, 6, 2, 5, 3, 4)
+PAIRS = ((1, 2), (3, 4), (5, 6), (0, 7))
 
 
 def kernel(
-    tok_hbm, grad_hbm, meta_hbm, gate_hbm, up_hbm, down_hbm,
+    tok_hbm, grad_hbm, ids_hbm, prob_hbm, gate_hbm, up_hbm, down_hbm,
     tok_out, gate_out, up_out, down_out,
-    tok, grad, meta, wgu, wd, send, recv, xs, gs, hid, giui, rsend, rrecv, selt,
-    zsend, zrecv, own, gu_send, gu_recv, d_send, d_recv,
-    load_sem, ring_s, ring_r, w_s, w_r, disp_s, disp_r, ret_s, ret_r, z_s, z_r, g_s, g_r,
+    ids_in, prob_in, result, tok, grad, meta, wgu, wd, send, recv, ssend, srecv, xs, gs, hid, giui, rsend, rrecv, selt,
+    zsend, zrecv, zhalf, own, gu_send, gu_recv, d_send, d_recv,
+    load_sem, store_sem, ring_s, ring_r, w_s, w_r, disp_s, disp_r, ret_s, ret_r, z_s, z_r, g_s, g_r,
 ):
     z = lax.axis_index("rep")
     e = lax.axis_index("exp")
@@ -45,7 +46,8 @@
         return ((z + d) % REP, e)
 
     loads = [
-        pltpu.make_async_copy(meta_hbm, meta.at[0], load_sem.at[0]),
+        pltpu.make_async_copy(ids_hbm, ids_in, load_sem.at[0]),
+        pltpu.make_async_copy(prob_hbm, prob_in, load_sem.at[6]),
         pltpu.make_async_copy(tok_hbm, tok.at[0], load_sem.at[1]),
         pltpu.make_async_copy(grad_hbm, grad.at[0], load_sem.at[2]),
         pltpu.make_async_copy(gate_hbm, wgu.at[:, pl.ds(0, HALF)], load_sem.at[3]),
@@ -84,17 +86,27 @@
 
     def pieces(direction, h):
         if h < 4:
-            return (2, 0, 1)
-        return ((2, 0), (1,))[direction]
-
-    for c in loads[:3]:
+            return (0, 1, 2)
+        return ((0, 2), (1,))[direction]
+
+    for c in loads[2:4]:
         c.wait()
-    for piece in (2, 0, 1):
+    for piece in (0, 1):
         for direction in (0, 1):
             hop(direction, 1, piece).start()
+    for c in loads[:2]:
+        c.wait()
+
+    def twice(values, fill):
+        return jnp.concatenate([values, values, jnp.full((TOP, 128 - 2 * ROWS), fill, F32)], axis=1)
+
+    meta[0, 0:8, :] = twice(ids_in[...].astype(F32), -1.0)
+    meta[0, 8:16, :] = twice(prob_in[...], 0.0)
+    for direction in (0, 1):
+        hop(direction, 1, 2).start()
 
     def advance(h):
-        for piece in (2, 0, 1):
+        for piece in (0, 1, 2):
             for direction in (0, 1):
                 if piece in pieces(direction, h):
                     hop(direction, h, piece).wait_recv()
@@ -113,10 +125,6 @@
             device_id=partner, device_id_type=MESH,
         )
 
-    for k in range(3):
-        loads[3 + k].wait()
-        weight_copy(k).start()
-
     row = lax.broadcasted_iota(jnp.int32, (128, 128), 0)
     lane = lax.broadcasted_iota(jnp.int32, (128, 128), 1)
     low = lane < ROWS
@@ -125,29 +133,37 @@
     expert = (16 * z + row // 8).astype(F32)
     rank = (row % 4).astype(F32)
 
+    def disp_refs(g):
+        if g < 3:
+            return send.at[g], recv.at[g]
+        return ssend.at[g - 3], srecv.at[g - 3]
+
     def disp(g, i):
         q = plane(i)
-        return pltpu.make_async_remote_copy(
-            src_ref=send.at[g, q], dst_ref=recv.at[g, p],
+        src, dst = disp_refs(g)
+        return pltpu.make_async_remote_copy(
+            src_ref=src.at[q], dst_ref=dst.at[p],
             send_sem=disp_s.at[g, q], recv_sem=disp_r.at[g, p],
             device_id=(z, q * 2 + core), device_id_type=MESH,
         )
 
     def disp_own(g):
-        return pltpu.make_async_copy(send.at[g, p], recv.at[g, p], disp_r.at[g, p])
+        src, dst = disp_refs(g)
+        return pltpu.make_async_copy(src.at[p], dst.at[p], disp_r.at[g, p])
 
     def disp_recv(g, i):
         q = plane(i)
-        return pltpu.make_async_remote_copy(
-            src_ref=send.at[g, q], dst_ref=recv.at[g, q],
+        src, dst = disp_refs(g)
+        return pltpu.make_async_remote_copy(
+            src_ref=src.at[q], dst_ref=dst.at[q],
             send_sem=disp_s.at[g, q], recv_sem=disp_r.at[g, q],
             device_id=(z, q * 2 + core), device_id_type=MESH,
         )
 
-    def dispatch(g):
+    def select(first, second):
         low8 = low[:8]
-        ids = jnp.where(low8, meta[2 * g, 0:8, :], meta[2 * g + 1, 0:8, :])
-        prob = jnp.where(low8, meta[2 * g, 8:16, :], meta[2 * g + 1, 8:16, :])
+        ids = jnp.where(low8, meta[first, 0:8, :], meta[second, 0:8, :])
+        prob = jnp.where(low8, meta[first, 8:16, :], meta[second, 8:16, :])
         hit = jnp.zeros((128, 128), F32)
         weight = jnp.zeros((128, 128), F32)
         for k in range(TOP):
@@ -157,21 +173,32 @@
         hit = jnp.where(same_chunk, hit, 0.0)
         before = jnp.dot(hit.astype(BF16), tri, preferred_element_type=F32)
         sel = jnp.where(before == rank, hit, 0.0)
-        scale = jnp.sum(sel * weight, axis=1, keepdims=True)
-        selt[g] = sel.T.astype(BF16)
+        return sel, jnp.sum(sel * weight, axis=1, keepdims=True)
+
+    def dispatch(g):
+        single = g >= 3
+        first, second = PAIRS[g] if not single else ((0, 0), (7, 7))[g - 3]
+        sel, scale = select(first, second)
+        if not single:
+            selt[g] = sel.T.astype(BF16)
         sel_rows = sel.astype(BF16)[:, : 2 * ROWS]
 
         def tile(j, carry):
             cols = pl.ds(pl.multiple_of(j * 512, 512), 512)
-            t2 = tok[2 * g : 2 * g + 2, :, cols].reshape(2 * ROWS, 512)
-            g2 = grad[2 * g : 2 * g + 2, :, cols].reshape(2 * ROWS, 512)
+            if single:
+                right = pl.ds(pl.multiple_of(j * 512 + 1024, 512), 512)
+                t2 = jnp.concatenate([tok[first, :, cols], tok[first, :, right]], axis=0)
+                g2 = jnp.concatenate([grad[first, :, cols], grad[first, :, right]], axis=0)
+            else:
+                t2 = tok[first : first + 2, :, cols].reshape(2 * ROWS, 512)
+                g2 = grad[first : first + 2, :, cols].reshape(2 * ROWS, 512)
             a = jnp.dot(sel_rows, t2, preferred_element_type=F32)
             b = jnp.dot(sel_rows, g2, preferred_element_type=F32) * scale
             both = jnp.concatenate([a.reshape(16, 8, 512), b.reshape(16, 8, 512)], axis=1)
-            send[g, :, :, cols] = both.astype(BF16)
-            return carry
-
-        lax.fori_loop(0, 4, tile, 0)
+            disp_refs(g)[0][:, :, cols] = both.astype(BF16)
+            return carry
+
+        lax.fori_loop(0, 2 if single else 4, tile, 0)
 
         def go(i, carry):
             disp(g, i).start()
@@ -199,23 +226,42 @@
             device_id=(z, q * 2 + core), device_id_type=MESH,
         )
 
+    def landed(g):
+        def wait(i, carry):
+            disp_recv(g, i).wait_recv()
+            return carry
+
+        lax.fori_loop(1, 16, wait, 0)
+        disp_own(g).wait()
+
     def expert_rows(g):
-        def landed(i, carry):
-            disp_recv(g, i).wait_recv()
-            return carry
-
-        lax.fori_loop(1, 16, landed, 0)
-        disp_own(g).wait()
         rows = pl.ds(g * 128, 128)
-
-        def unpack(j, carry):
-            cols = pl.ds(pl.multiple_of(j * 512, 512), 512)
-            both = recv[g, :, :, cols].astype(F32)
-            xs[rows, cols] = both[:, 0:8].reshape(128, 512).astype(BF16)
-            gs[rows, cols] = both[:, 8:16].reshape(128, 512).astype(BF16)
-            return carry
-
-        lax.fori_loop(0, 4, unpack, 0)
+        landed(g)
+        if g < 3:
+            def unpack(j, carry):
+                cols = pl.ds(pl.multiple_of(j * 512, 512), 512)
+                both = recv[g, :, :, cols].astype(F32)
+                xs[rows, cols] = both[:, 0:8].reshape(128, 512).astype(BF16)
+                gs[rows, cols] = both[:, 8:16].reshape(128, 512).astype(BF16)
+                return carry
+
+            lax.fori_loop(0, 4, unpack, 0)
+        else:
+            landed(4)
+
+            def unpack(j, carry):
+                left = pl.multiple_of(j * 256, 256)
+                near = srecv[0, :, :, pl.ds(left, 256)].astype(F32)
+                far = srecv[1, :, :, pl.ds(left, 256)].astype(F32)
+                for side in range(2):
+                    cols = pl.ds(left + side * 1024, 256)
+                    for out, base in ((xs, 0), (gs, 8)):
+                        lo = base + 4 * side
+                        both = jnp.concatenate([near[:, lo : lo + 4], far[:, lo : lo + 4]], axis=1)
+                        out[rows, cols] = both.reshape(128, 256).astype(BF16)
+                return carry
+
+            lax.fori_loop(0, 4, unpack, 0)
         if g == 0:
             for k in range(3):
                 weight_copy(k).wait_recv()
@@ -247,6 +293,7 @@
 
         lax.fori_loop(0, 2, back, 0)
 
+    def send_back(g):
         def go(i, carry):
             ret(g, i).start()
             return carry
@@ -254,38 +301,54 @@
         lax.fori_loop(1, 16, go, 0)
         ret_own(g).start()
 
-    def zcopy(j):
-        return pltpu.make_async_remote_copy(
-            src_ref=zsend.at[j], dst_ref=zrecv.at[j],
-            send_sem=z_s.at[j], recv_sem=z_r.at[j],
-            device_id=zdev(OFFSET[j]), device_id_type=MESH,
+    def ways(h, block):
+        return (0, 1) if h < 4 else (block // 2,)
+
+    def inward(direction, h, block):
+        cols = pl.ds(block * 512, 512)
+        if h == 4:
+            dst = zhalf.at[:, cols]
+        else:
+            dst = zrecv.at[direction, h - 1, :, cols]
+        return pltpu.make_async_remote_copy(
+            src_ref=zsend.at[(UP, DOWN)[direction][h], :, cols], dst_ref=dst,
+            send_sem=z_s.at[direction, h - 1, block], recv_sem=z_r.at[direction, h - 1, block],
+            device_id=zdev((7, 1)[direction]), device_id_type=MESH,
         )
 
     def combine(g):
-        def landed(i, carry):
+        first, second = PAIRS[g]
+
+        def wait(i, carry):
             ret_recv(g, i).wait_recv()
             return carry
 
-        lax.fori_loop(1, 16, landed, 0)
+        lax.fori_loop(1, 16, wait, 0)
         ret_own(g).wait()
-
-        def tile(j, carry):
-            both = rrecv[g, :, :, pl.ds(pl.multiple_of(j * 512, 512), 512)].astype(F32)
-            for side in range(2):
-                cols = pl.ds(pl.multiple_of(j * 512 + side * 1024, 512), 512)
-                part = both[:, side * 8 : side * 8 + 8].reshape(128, 512).astype(BF16)
-                total = jnp.dot(selt[g], part, preferred_element_type=F32)
-                if g == 0:
-                    own[:, cols] = total[:ROWS]
-                else:
-                    zsend[2 * g, :, cols] = total[:ROWS].astype(BF16)
-                zsend[2 * g + 1, :, cols] = total[ROWS : 2 * ROWS].astype(BF16)
-            return carry
-
-        lax.fori_loop(0, 2, tile, 0)
-        for j in (2 * g + 1, 2 * g):
-            if j > 0:
-                zcopy(j).start()
+        for block in (0, 2, 1, 3):
+            cols = pl.ds(block * 512, 512)
+            narrow = pl.ds(block % 2 * 512, 512)
+            side = block // 2
+            part = rrecv[g, :, :, narrow].astype(F32)[:, side * 8 : side * 8 + 8]
+            total = jnp.dot(selt[g], part.reshape(128, 512).astype(BF16), preferred_element_type=F32)
+            near, far = total[:ROWS], total[ROWS : 2 * ROWS]
+            if g < 3:
+                for direction in ways(g + 2, block):
+                    inward(direction, g + 2, block).wait_recv()
+            if g < 2:
+                near = near + zrecv[0, g + 1, :, cols].astype(F32)
+                far = far + zrecv[1, g + 1, :, cols].astype(F32)
+            elif g == 2 and side == 0:
+                near = near + zhalf[:, cols].astype(F32)
+            elif g == 2:
+                far = far + zhalf[:, cols].astype(F32)
+            if g < 3:
+                zsend[first, :, cols] = near.astype(BF16)
+            else:
+                own[:, cols] = near
+            zsend[second, :, cols] = far.astype(BF16)
+            for direction in ways(g + 1, block):
+                inward(direction, g + 1, block).start()
 
     def grad_copy(k):
         src, dst = ((gu_send.at[0], gu_recv.at[0]), (gu_send.at[1], gu_recv.at[1]), (d_send, d_recv))[k]
@@ -325,57 +388,69 @@
         lax.fori_loop(0, 4, tile_down, 0)
         grad_copy(2).start()
 
+    def store(k):
+        src, dst = (
+            (gu_recv.at[0], gate_out), (gu_recv.at[1], up_out), (d_recv, down_out), (result, tok_out)
+        )[k]
+        return pltpu.make_async_copy(src, dst, store_sem.at[k])
+
     def own_grads():
         grad_copy(0).wait_recv()
         grad_copy(1).wait_recv()
 
         def tile(j, carry):
             rows, both = gate_up_tile(j, 0)
-            gate_out[rows, :] = (both[:, :HALF] + gu_recv[0, rows, :].astype(F32)).astype(BF16)
-            up_out[rows, :] = (both[:, HALF:] + gu_recv[1, rows, :].astype(F32)).astype(BF16)
+            gu_recv[0, rows, :] = (both[:, :HALF] + gu_recv[0, rows, :].astype(F32)).astype(BF16)
+            gu_recv[1, rows, :] = (both[:, HALF:] + gu_recv[1, rows, :].astype(F32)).astype(BF16)
             return carry
 
         lax.fori_loop(0, 8, tile, 0)
+        store(0).start()
+        store(1).start()
         grad_copy(2).wait_recv()
 
         def tile_down(j, carry):
             cols, part = down_tile(j, 0)
-            down_out[:, cols] = (part + d_recv[:, cols].astype(F32)).astype(BF16)
+            d_recv[:, cols] = (part + d_recv[:, cols].astype(F32)).astype(BF16)
             return carry
 
         lax.fori_loop(0, 4, tile_down, 0)
-
+        store(2).start()
+
+    dispatch(3)
+    for k in range(3):
+        loads[4 + k].wait()
+        weight_copy(k).start()
     advance(1)
     dispatch(0)
     advance(2)
     dispatch(1)
-    expert_rows(0)
     advance(3)
     dispatch(2)
+    advance(4)
+    dispatch(4)
+    selt[3] = select(*PAIRS[3])[0].T.astype(BF16)
+    expert_rows(0)
     expert_rows(1)
-    advance(4)
-    dispatch(3)
+    expert_rows(2)
+    send_back(2)
+    expert_rows(3)
+    send_back(3)
+    send_back(1)
+    send_back(0)
+    partner_grads()
+    combine(3)
+    combine(2)
+    combine(1)
     combine(0)
-    expert_rows(2)
-    combine(1)
-    expert_rows(3)
-    partner_grads()
-    combine(2)
-    combine(3)
     own_grads()
-
-    for j in range(1, REP):
-        zcopy(j).wait_recv()
-
-    def finish(j, carry):
-        cols = pl.ds(pl.multiple_of(j * 512, 512), 512)
-        total = own[:, cols]
-        for k in range(1, REP):
-            total = total + zrecv[k, :, cols].astype(F32)
-        tok_out[:, cols] = total.astype(BF16)
-        return carry
-
-    lax.fori_loop(0, 4, finish, 0)
+    for block in (0, 2, 1, 3):
+        cols = pl.ds(block * 512, 512)
+        for direction in (0, 1):
+            inward(direction, 1, block).wait_recv()
+        total = own[:, cols] + zrecv[0, 0, :, cols].astype(F32) + zrecv[1, 0, :, cols].astype(F32)
+        result[:, cols] = total.astype(BF16)
+    store(3).start()
 
     for h in range(1, 5):
         for direction in (0, 1):
@@ -384,27 +459,25 @@
     for k in range(3):
         weight_copy(k).wait_send()
         grad_copy(k).wait_send()
-    for j in range(1, REP):
-        zcopy(j).wait_send()
+    for h in range(1, 5):
+        for block in range(4):
+            for direction in ways(h, block):
+                inward(direction, h, block).wait_send()
 
     def drain(i, carry):
+        for g in range(GROUPS + 1):
+            disp(g, i).wait_send()
         for g in range(GROUPS):
-            disp(g, i).wait_send()
             ret(g, i).wait_send()
         return carry
 
     lax.fori_loop(1, 16, drain, 0)
+    for k in range(4):
+        store(k).wait()
 
 
 def per_device(tokens, grad_out, expert_ids, gate_probs, gate_weight, up_weight, down_weight):
-    def lay(values, fill):
-        t = values.astype(F32).T
-        pad = jnp.full((TOP, 128 - 2 * ROWS), fill, F32)
-        return jnp.concatenate([t, t, pad], axis=1)
-
-    meta = jnp.concatenate([lay(expert_ids, -1.0), lay(gate_probs, 0.0)], axis=0)
     anywhere = pl.BlockSpec(memory_space=pl.ANY)
-    vmem = pl.BlockSpec(memory_space=pltpu.VMEM)
     dma = pltpu.SemaphoreType.DMA
     tok_grad, gate_grad, up_grad, down_grad = pl.pallas_call(
         kernel,
@@ -414,16 +487,21 @@
             jax.ShapeDtypeStruct((D, HALF), BF16),
             jax.ShapeDtypeStruct((HALF, D), BF16),
         ),
-        in_specs=[anywhere] * 6,
-        out_specs=[vmem] * 4,
+        in_specs=[pl.BlockSpec(memory_space=pltpu.HBM)] * 7,
+        out_specs=[anywhere] * 4,
         scratch_shapes=[
+            pltpu.VMEM((TOP, ROWS), jnp.int32),
+            pltpu.VMEM((TOP, ROWS), F32),
+            pltpu.VMEM((ROWS, D), BF16),
             pltpu.VMEM((REP, ROWS, D), BF16),
             pltpu.VMEM((REP, ROWS, D), BF16),
             pltpu.VMEM((REP, 16, 128), F32),
             pltpu.VMEM((D, 4 * HALF), BF16),
             pltpu.VMEM((2 * HALF, D), BF16),
-            pltpu.VMEM((GROUPS, 16, 16, D), BF16),
-            pltpu.VMEM((GROUPS, 16, 16, D), BF16),
+            pltpu.VMEM((3, 16, 16, D), BF16),
+            pltpu.VMEM((3, 16, 16, D), BF16),
+            pltpu.VMEM((2, 16, 16, D // 2), BF16),
+            pltpu.VMEM((2, 16, 16, D // 2), BF16),
             pltpu.VMEM((GROUPS * 128, D), BF16),
             pltpu.VMEM((GROUPS * 128, D), BF16),
             pltpu.VMEM((GROUPS * 128, 2 * HALF), BF16),
@@ -432,30 +510,37 @@
             pltpu.VMEM((GROUPS, 16, 16, D // 2), BF16),
             pltpu.VMEM((GROUPS, 128, 128), BF16),
             pltpu.VMEM((REP, ROWS, D), BF16),
-            pltpu.VMEM((REP, ROWS, D), BF16),
+            pltpu.VMEM((2, 3, ROWS, D), BF16),
+            pltpu.VMEM((ROWS, D), BF16),
             pltpu.VMEM((ROWS, D), F32),
             pltpu.VMEM((2, D, HALF), BF16),
             pltpu.VMEM((2, D, HALF), BF16),
             pltpu.VMEM((HALF, D), BF16),
             pltpu.VMEM((HALF, D), BF16),
-            dma((6,)),
+            dma((7,)),
+            dma((4,)),
             dma((2, 4, 3)),
             dma((2, 4, 3)),
             dma((3,)),
             dma((3,)),
+            dma((GROUPS + 1, 16)),
+            dma((GROUPS + 1, 16)),
             dma((GROUPS, 16)),
             dma((GROUPS, 16)),
-            dma((GROUPS, 16)),
-            dma((GROUPS, 16)),
-            dma((REP,)),
-            dma((REP,)),
+            dma((2, 4, 4)),
+            dma((2, 4, 4)),
             dma((3,)),
             dma((3,)),
         ],
         compiler_params=pltpu.CompilerParams(
-            collective_id=0, has_side_effects=True, vmem_limit_bytes=60 * 2**20
+            collective_id=0, has_side_effects=True, vmem_limit_bytes=LIMIT * 2**20
         ),
-    )(tokens, grad_out, meta, gate_weight[0], up_weight[0], down_weight[0])
+    )(*(
+        pltpu.with_memory_space_constraint(x, pltpu.HBM)
+        for x in (
+            tokens, grad_out, expert_ids.T, gate_probs.T, gate_weight[0], up_weight[0], down_weight[0]
+        )
+    ))
     return tok_grad, gate_grad[None], up_grad[None], down_grad[None]
 
 

time: 136 us -> 111 us (0.82)
  Pallas kernels: 125 us -> 105 us
  local copies, waits for them, and re-layouts: 7.57 us -> 4.11 us
  other arithmetic: 2.13 us -> 0 us
    pallas_call x1, Pallas kernels: 125 us -> 105 us  [per_device(): pl.pallas_call(kernel, out_shape=(jax.ShapeDtypeStruct((ROWS, D), BF16),...]
    unnamed x8 -> x4, local copies, waits for them, and re-layouts: 7.56 us -> 4.11 us
    concatenate x1 -> x0, other arithmetic: 1.44 us -> none  [per_device(): jnp.concatenate([lay(expert_ids, -1.0), lay(gate_probs, 0.0)], axis=0)]
where the time goes in v2:
time: 111 us; the launch traced here: 110 us
  Pallas kernels  105 us (95%)
  local copies, waits for them, and re-layouts  4.11 us (4%)
    pallas_call x1, Pallas kernels, per_device(): pl.pallas_call(kernel, out_shape=(jax.ShapeDtypeStruct((ROWS, D), BF16),...  105 us
    unnamed x4, local copies, waits for them, and re-layouts  4.11 us

profile of v2, /device:TPU:8, one launch (start us, length us, event | category | flops | bytes accessed | tf_op | source)
XLA Modules:
  0.0 110.0 jit_solution(10701743384615239763)
XLA Ops:
  0.6 105.2 %shard_map.102 = (bf16[48,2048]{1,0:T(8,128)(2,1)S(1)}, bf16[2048,384]{1,0:T(8,128)(2,1)S(1)}, bf16[2048,384]{1,0:T(8,128)(2,1)S(1)}, bf16[384,2048]{1,0:T(8,128)(2,1)S(1)}) custom-call(bf16[48,2048]{1,0:T(8,128)(2,1)} %tok_hbm.1, bf16[48,2048]{1,0:T(8,128)(2,1)} %grad_hbm.1, s32[8,48]{1,0:T(8,128)} %bitcast.14, f32[8,48]{1,0:T(8,128)} %bitcast.15, ...), custom_call_target="tpu_custom_call" | custom-call | tf_op jit(solution)/shard_map/pallas_call | solution.py:482
  105.9 0.7 copy.15
  106.6 1.1 %copy.16 = bf16[1,2048,384]{2,1,0:T(8,128)(2,1)} copy(bf16[1,2048,384]{2,1,0:T(8,128)(2,1)S(1)} %bitcast.10) | data formatting | bytes 3145728
  107.7 1.1 %copy.17 = bf16[1,2048,384]{2,1,0:T(8,128)(2,1)} copy(bf16[1,2048,384]{2,1,0:T(8,128)(2,1)S(1)} %bitcast.9) | data formatting | bytes 3145728
  108.8 1.1 %copy.18 = bf16[1,384,2048]{2,1,0:T(8,128)(2,1)} copy(bf16[1,384,2048]{2,1,0:T(8,128)(2,1)S(1)} %bitcast.8) | data formatting | bytes 3145728

commit v3 on v2

--- a/solution.py
+++ b/solution.py
@@ -27,7 +27,7 @@
 def kernel(
     tok_hbm, grad_hbm, ids_hbm, prob_hbm, gate_hbm, up_hbm, down_hbm,
     tok_out, gate_out, up_out, down_out,
-    ids_in, prob_in, result, tok, grad, meta, wgu, wd, send, recv, ssend, srecv, xs, gs, hid, giui, rsend, rrecv, selt,
+    ids_in, prob_in, result, tok, grad, meta, wgu, wd, send, recv, ssend, srecv, xs, gs, hid, giui, rsend, rrecv, srsend, srrecv, selt,
     zsend, zrecv, zhalf, own, gu_send, gu_recv, d_send, d_recv,
     load_sem, store_sem, ring_s, ring_r, w_s, w_r, disp_s, disp_r, ret_s, ret_r, z_s, z_r, g_s, g_r,
 ):
@@ -91,22 +91,22 @@
 
     for c in loads[2:4]:
         c.wait()
-    for piece in (0, 1):
+    for direction in (0, 1):
+        hop(direction, 1, 0).start()
+    for c in loads[:2]:
+        c.wait()
+
+    def twice(values, fill):
+        return jnp.concatenate([values, values, jnp.full((TOP, 128 - 2 * ROWS), fill, F32)], axis=1)
+
+    meta[0, 0:8, :] = twice(ids_in[...].astype(F32), -1.0)
+    meta[0, 8:16, :] = twice(prob_in[...], 0.0)
+    for piece in (2, 1):
         for direction in (0, 1):
             hop(direction, 1, piece).start()
-    for c in loads[:2]:
-        c.wait()
-
-    def twice(values, fill):
-        return jnp.concatenate([values, values, jnp.full((TOP, 128 - 2 * ROWS), fill, F32)], axis=1)
-
-    meta[0, 0:8, :] = twice(ids_in[...].astype(F32), -1.0)
-    meta[0, 8:16, :] = twice(prob_in[...], 0.0)
-    for direction in (0, 1):
-        hop(direction, 1, 2).start()
-
-    def advance(h):
-        for piece in (0, 1, 2):
+
+    def advance(h, chosen=(0, 2, 1)):
+        for piece in chosen:
             for direction in (0, 1):
                 if piece in pieces(direction, h):
                     hop(direction, h, piece).wait_recv()
@@ -134,9 +134,10 @@
     rank = (row % 4).astype(F32)
 
     def disp_refs(g):
-        if g < 3:
-            return send.at[g], recv.at[g]
-        return ssend.at[g - 3], srecv.at[g - 3]
+        if g in (1, 2):
+            return send.at[g - 1], recv.at[g - 1]
+        slot = {3: 0, 4: 1, 0: 2, 5: 3}[g]
+        return ssend.at[slot], srecv.at[slot]
 
     def disp(g, i):
         q = plane(i)
@@ -175,6 +176,14 @@
         sel = jnp.where(before == rank, hit, 0.0)
         return sel, jnp.sum(sel * weight, axis=1, keepdims=True)
 
+    def launch(g):
+        def go(i, carry):
+            disp(g, i).start()
+            return carry
+
+        lax.fori_loop(1, 16, go, 0)
+        disp_own(g).start()
+
     def dispatch(g):
         single = g >= 3
         first, second = PAIRS[g] if not single else ((0, 0), (7, 7))[g - 3]
@@ -199,29 +208,48 @@
             return carry
 
         lax.fori_loop(0, 2 if single else 4, tile, 0)
-
-        def go(i, carry):
-            disp(g, i).start()
-            return carry
-
-        lax.fori_loop(1, 16, go, 0)
-        disp_own(g).start()
+        launch(g)
+
+    def dispatch_near(message, buf, sel_rows, scale):
+        def tile(j, carry):
+            cols = pl.ds(pl.multiple_of(j * 512, 512), 512)
+            halves = []
+            for side in range(2):
+                from_cols = pl.ds(pl.multiple_of(j * 512 + side * 1024, 512), 512)
+                rows2 = buf[1:3, :, from_cols].reshape(2 * ROWS, 512)
+                part = jnp.dot(sel_rows, rows2, preferred_element_type=F32)
+                if scale is not None:
+                    part = part * scale
+                halves.append(part.reshape(16, 8, 512))
+            disp_refs(message)[0][:, :, cols] = jnp.concatenate(halves, axis=1).astype(BF16)
+            return carry
+
+        lax.fori_loop(0, 2, tile, 0)
+        launch(message)
+
+    def ret_refs(g):
+        if g < 3:
+            return rsend.at[g], rrecv.at[g]
+        return srsend.at[g - 3], srrecv.at[g - 3]
 
     def ret(g, i):
         q = plane(i)
-        return pltpu.make_async_remote_copy(
-            src_ref=rsend.at[g, q], dst_ref=rrecv.at[g, p],
+        src, dst = ret_refs(g)
+        return pltpu.make_async_remote_copy(
+            src_ref=src.at[q], dst_ref=dst.at[p],
             send_sem=ret_s.at[g, q], recv_sem=ret_r.at[g, p],
             device_id=(z, q * 2 + core), device_id_type=MESH,
         )
 
     def ret_own(g):
-        return pltpu.make_async_copy(rsend.at[g, p], rrecv.at[g, p], ret_r.at[g, p])
+        src, dst = ret_refs(g)
+        return pltpu.make_async_copy(src.at[p], dst.at[p], ret_r.at[g, p])
 
     def ret_recv(g, i):
         q = plane(i)
-        return pltpu.make_async_remote_copy(
-            src_ref=rsend.at[g, q], dst_ref=rrecv.at[g, q],
+        src, dst = ret_refs(g)
+        return pltpu.make_async_remote_copy(
+            src_ref=src.at[q], dst_ref=dst.at[q],
             send_sem=ret_s.at[g, q], recv_sem=ret_r.at[g, q],
             device_id=(z, q * 2 + core), device_id_type=MESH,
         )
@@ -237,10 +265,22 @@
     def expert_rows(g):
         rows = pl.ds(g * 128, 128)
         landed(g)
-        if g < 3:
+        if g == 0:
+            landed(5)
+
+            def unpack(j, carry):
+                left = pl.multiple_of(j * 512, 512)
+                for slot, out in ((2, xs), (3, gs)):
+                    both = srecv[slot, :, :, pl.ds(left, 512)].astype(F32)
+                    out[rows, pl.ds(left, 512)] = both[:, 0:8].reshape(128, 512).astype(BF16)
+                    out[rows, pl.ds(left + 1024, 512)] = both[:, 8:16].reshape(128, 512).astype(BF16)
+                return carry
+
+            lax.fori_loop(0, 2, unpack, 0)
+        elif g < 3:
             def unpack(j, carry):
                 cols = pl.ds(pl.multiple_of(j * 512, 512), 512)
-                both = recv[g, :, :, cols].astype(F32)
+                both = recv[g - 1, :, :, cols].astype(F32)
                 xs[rows, cols] = both[:, 0:8].reshape(128, 512).astype(BF16)
                 gs[rows, cols] = both[:, 8:16].reshape(128, 512).astype(BF16)
                 return carry
@@ -282,6 +322,22 @@
 
         lax.fori_loop(0, 2, forward, 0)
 
+        if g == 3:
+            def back_single(j, carry):
+                cols = pl.ds(pl.multiple_of(j * 256, 256), 256)
+                parts = []
+                for q in range(4):
+                    feats = pl.ds(pl.multiple_of(j * 256 + q * 512, 256), 256)
+                    a = lax.dot_general(giui[rows, :], wgu[feats, :], NT, preferred_element_type=F32)
+                    parts.append(a.reshape(16, 8, 256))
+                for c in range(2):
+                    packed = jnp.concatenate([a[:, c * 4 : c * 4 + 4] for a in parts], axis=1)
+                    srsend[c, :, :, cols] = packed.astype(BF16)
+                return carry
+
+            lax.fori_loop(0, 2, back_single, 0)
+            return
+
         def back(j, carry):
             out = pl.ds(pl.multiple_of(j * 512, 512), 512)
             right = pl.ds(pl.multiple_of(j * 512 + 1024, 512), 512)
@@ -316,15 +372,31 @@
             device_id=zdev((7, 1)[direction]), device_id_type=MESH,
         )
 
+    def returned(g):
+        def wait(i, carry):
+            ret_recv(g, i).wait_recv()
+            return carry
+
+        lax.fori_loop(1, 16, wait, 0)
+        ret_own(g).wait()
+
+    def combine_single(c):
+        returned(3 + c)
+        for block in (0, 2, 1, 3):
+            cols = pl.ds(block * 512, 512)
+            part = srrecv[c, :, :, :].astype(F32)[:, block * 4 : block * 4 + 4]
+            part = jnp.concatenate([part, part], axis=1).reshape(128, 512).astype(BF16)
+            total = jnp.dot(selt[3], part, preferred_element_type=F32)
+            if c == 0:
+                own[:, cols] = total[:ROWS]
+            else:
+                zsend[7, :, cols] = total[ROWS : 2 * ROWS].astype(BF16)
+                for direction in ways(4, block):
+                    inward(direction, 4, block).start()
+
     def combine(g):
         first, second = PAIRS[g]
-
-        def wait(i, carry):
-            ret_recv(g, i).wait_recv()
-            return carry
-
-        lax.fori_loop(1, 16, wait, 0)
-        ret_own(g).wait()
+        returned(g)
         for block in (0, 2, 1, 3):
             cols = pl.ds(block * 512, 512)
             narrow = pl.ds(block % 2 * 512, 512)
@@ -332,22 +404,18 @@
             part = rrecv[g, :, :, narrow].astype(F32)[:, side * 8 : side * 8 + 8]
             total = jnp.dot(selt[g], part.reshape(128, 512).astype(BF16), preferred_element_type=F32)
             near, far = total[:ROWS], total[ROWS : 2 * ROWS]
-            if g < 3:
-                for direction in ways(g + 2, block):
-                    inward(direction, g + 2, block).wait_recv()
+            for direction in ways(g + 2, block):
+                inward(direction, g + 2, block).wait_recv()
             if g < 2:
                 near = near + zrecv[0, g + 1, :, cols].astype(F32)
                 far = far + zrecv[1, g + 1, :, cols].astype(F32)
-            elif g == 2 and side == 0:
+            elif side == 0:
                 near = near + zhalf[:, cols].astype(F32)
-            elif g == 2:
+            else:
                 far = far + zhalf[:, cols].astype(F32)
-            if g < 3:
-                zsend[first, :, cols] = near.astype(BF16)
-            else:
-                own[:, cols] = near
+            zsend[first, :, cols] = near.astype(BF16)
             zsend[second, :, cols] = far.astype(BF16)
-            for direction in ways(g + 1, block):
+            for direction in (0, 1):
                 inward(direction, g + 1, block).start()
 
     def grad_copy(k):
@@ -421,8 +489,13 @@
     for k in range(3):
         loads[4 + k].wait()
         weight_copy(k).start()
-    advance(1)
-    dispatch(0)
+    advance(1, (0, 2))
+    near_sel, near_scale = select(1, 2)
+    selt[0] = near_sel.T.astype(BF16)
+    near_rows = near_sel.astype(BF16)[:, : 2 * ROWS]
+    dispatch_near(0, tok, near_rows, None)
+    advance(1, (1,))
+    dispatch_near(5, grad, near_rows, near_scale)
     advance(2)
     dispatch(1)
     advance(3)
@@ -435,15 +508,17 @@
     expert_rows(2)
     send_back(2)
     expert_rows(3)
-    send_back(3)
+    send_back(4)
     send_back(1)
     send_back(0)
+    send_back(3)
     partner_grads()
-    combine(3)
+    combine_single(1)
     combine(2)
     combine(1)
     combine(0)
     own_grads()
+    combine_single(0)
     for block in (0, 2, 1, 3):
         cols = pl.ds(block * 512, 512)
         for direction in (0, 1):
@@ -465,15 +540,24 @@
                 inward(direction, h, block).wait_send()
 
     def drain(i, carry):
-        for g in range(GROUPS + 1):
+        for g in range(6):
             disp(g, i).wait_send()
-        for g in range(GROUPS):
+        for g in range(5):
             ret(g, i).wait_send()
         return carry
 
     lax.fori_loop(1, 16, drain, 0)
     for k in range(4):
         store(k).wait()
+
+
+def store_out(*refs):
+    sems = refs[8]
+    copies = [pltpu.make_async_copy(refs[k], refs[4 + k], sems.at[k]) for k in range(4)]
+    for c in copies:
+        c.start()
+    for c in copies:
+        c.wait()
 
 
 def per_device(tokens, grad_out, expert_ids, gate_probs, gate_weight, up_weight, down_weight):
@@ -498,16 +582,18 @@
             pltpu.VMEM((REP, 16, 128), F32),
             pltpu.VMEM((D, 4 * HALF), BF16),
             pltpu.VMEM((2 * HALF, D), BF16),
-            pltpu.VMEM((3, 16, 16, D), BF16),
-            pltpu.VMEM((3, 16, 16, D), BF16),
-            pltpu.VMEM((2, 16, 16, D // 2), BF16),
-            pltpu.VMEM((2, 16, 16, D // 2), BF16),
+            pltpu.VMEM((2, 16, 16, D), BF16),
+            pltpu.VMEM((2, 16, 16, D), BF16),
+            pltpu.VMEM((4, 16, 16, D // 2), BF16),
+            pltpu.VMEM((4, 16, 16, D // 2), BF16),
             pltpu.VMEM((GROUPS * 128, D), BF16),
             pltpu.VMEM((GROUPS * 128, D), BF16),
             pltpu.VMEM((GROUPS * 128, 2 * HALF), BF16),
             pltpu.VMEM((GROUPS * 128, 4 * HALF), BF16),
-            pltpu.VMEM((GROUPS, 16, 16, D // 2), BF16),
-            pltpu.VMEM((GROUPS, 16, 16, D // 2), BF16),
+            pltpu.VMEM((3, 16, 16, D // 2), BF16),
+            pltpu.VMEM((3, 16, 16, D // 2), BF16),
+            pltpu.VMEM((2, 16, 16, D // 4), BF16),
+            pltpu.VMEM((2, 16, 16, D // 4), BF16),
             pltpu.VMEM((GROUPS, 128, 128), BF16),
             pltpu.VMEM((REP, ROWS, D), BF16),
             pltpu.VMEM((2, 3, ROWS, D), BF16),
@@ -523,10 +609,10 @@
             dma((2, 4, 3)),
             dma((3,)),
             dma((3,)),
-            dma((GROUPS + 1, 16)),
-            dma((GROUPS + 1, 16)),
-            dma((GROUPS, 16)),
-            dma((GROUPS, 16)),
+            dma((6, 16)),
+            dma((6, 16)),
+            dma((5, 16)),
+            dma((5, 16)),
             dma((2, 4, 4)),
             dma((2, 4, 4)),
             dma((3,)),
@@ -541,6 +627,15 @@
             tokens, grad_out, expert_ids.T, gate_probs.T, gate_weight[0], up_weight[0], down_weight[0]
         )
     ))
+    outs = (tok_grad, gate_grad, up_grad, down_grad)
+    tok_grad, gate_grad, up_grad, down_grad = pl.pallas_call(
+        store_out,
+        out_shape=tuple(jax.ShapeDtypeStruct(x.shape, x.dtype) for x in outs),
+        in_specs=[anywhere] * 4,
+        out_specs=[anywhere] * 4,
+        scratch_shapes=[dma((4,))],
+        compiler_params=pltpu.CompilerParams(vmem_limit_bytes=2**20),
+    )(*outs)
     return tok_grad, gate_grad[None], up_grad[None], down_grad[None]
 
 

time: 111 us -> 105 us (0.946)
  local copies, waits for them, and re-layouts: 4.11 us -> 0 us
    unnamed x4 -> x0, local copies, waits for them, and re-layouts: 4.11 us -> none
    pallas_call x1, Pallas kernels: 105 us -> 101 us  [per_device(): pl.pallas_call(kernel, out_shape=(jax.ShapeDtypeStruct((ROWS, D), BF16),...]
    pallas_call x0 -> x1, Pallas kernels: none -> 2.28 us  [per_device(): pl.pallas_call(store_out, out_shape=tuple((jax.ShapeDtypeStruct(x.shape,...]
where the time goes in v3:
time: 105 us; the launch traced here: 104 us
  Pallas kernels  104 us (99%)
    pallas_call x1, Pallas kernels, per_device(): pl.pallas_call(kernel, out_shape=(jax.ShapeDtypeStruct((ROWS, D), BF16),...  101 us
    pallas_call x1, Pallas kernels, per_device(): pl.pallas_call(store_out, out_shape=tuple((jax.ShapeDtypeStruct(x.shape,...  2.28 us

profile of v3, /device:TPU:8, one launch (start us, length us, event | category | flops | bytes accessed | tf_op | source)
XLA Modules:
  0.0 104.2 jit_solution(11806896282606230356)
XLA Ops:
  0.6 101.2 %shard_map.102 = (bf16[48,2048]{1,0:T(8,128)(2,1)S(1)}, bf16[2048,384]{1,0:T(8,128)(2,1)S(1)}, bf16[2048,384]{1,0:T(8,128)(2,1)S(1)}, bf16[384,2048]{1,0:T(8,128)(2,1)S(1)}) custom-call(bf16[48,2048]{1,0:T(8,128)(2,1)} %tok_hbm.1, bf16[48,2048]{1,0:T(8,128)(2,1)} %grad_hbm.1, s32[8,48]{1,0:T(8,128)} %bitcast.11, f32[8,48]{1,0:T(8,128)} %bitcast.12, ...), custom_call_target="tpu_custom_call" | custom-call | tf_op jit(solution)/shard_map/pallas_call | solution.py:566
  101.9 2.3 %shard_map.103 = (bf16[48,2048]{1,0:T(8,128)(2,1)}, bf16[2048,384]{1,0:T(8,128)(2,1)}, bf16[2048,384]{1,0:T(8,128)(2,1)}, bf16[384,2048]{1,0:T(8,128)(2,1)}) custom-call(bf16[48,2048]{1,0:T(8,128)(2,1)S(1)} %get-tuple-element.12.refs_0_, bf16[2048,384]{1,0:T(8,128)(2,1)S(1)} %get-tuple-element.13.refs_1_, bf16[2048,384]{1,0:T(8,128)(2,1)S(1)} %get-tuple-element.14.refs_2_, ...), custom_call_target="tpu_custom_call" | custom-call | tf_op jit(solution)/shard_map/pallas_call | solution.py:631

commit v4 on v3

--- a/solution.py
+++ b/solution.py
@@ -14,7 +14,7 @@
 HALF = 384
 TOP = 8
 GROUPS = 4
-LIMIT = 47
+LIMIT = 44
 NT = (((1,), (1,)), ((), ()))
 TN = (((0,), (0,)), ((), ()))
 
@@ -28,7 +28,7 @@
     tok_hbm, grad_hbm, ids_hbm, prob_hbm, gate_hbm, up_hbm, down_hbm,
     tok_out, gate_out, up_out, down_out,
     ids_in, prob_in, result, tok, grad, meta, wgu, wd, send, recv, ssend, srecv, xs, gs, hid, giui, rsend, rrecv, srsend, srrecv, selt,
-    zsend, zrecv, zhalf, own, gu_send, gu_recv, d_send, d_recv,
+    zsend, zrecv, zhalf, own, gu_recv, d_recv,
     load_sem, store_sem, ring_s, ring_r, w_s, w_r, disp_s, disp_r, ret_s, ret_r, z_s, z_r, g_s, g_r,
 ):
     z = lax.axis_index("rep")
@@ -419,38 +419,35 @@
                 inward(direction, g + 1, block).start()
 
     def grad_copy(k):
-        src, dst = ((gu_send.at[0], gu_recv.at[0]), (gu_send.at[1], gu_recv.at[1]), (d_send, d_recv))[k]
+        src, dst = (
+            (wgu.at[:, pl.ds(2 * HALF, HALF)], gu_recv.at[0]),
+            (wgu.at[:, pl.ds(3 * HALF, HALF)], gu_recv.at[1]),
+            (wd.at[pl.ds(HALF, HALF)], d_recv),
+        )[k]
         return pltpu.make_async_remote_copy(
             src_ref=src, dst_ref=dst, send_sem=g_s.at[k], recv_sem=g_r.at[k],
             device_id=partner, device_id_type=MESH,
         )
 
-    def gate_up_tile(j, h):
-        rows = pl.ds(pl.multiple_of(j * 256, 256), 256)
-        return rows, lax.dot_general(
-            xs[:, rows], giui[:, h * 2 * HALF : (h + 1) * 2 * HALF], TN, preferred_element_type=F32
-        )
-
-    def down_tile(j, h):
-        cols = pl.ds(pl.multiple_of(j * 512, 512), 512)
-        return cols, lax.dot_general(
-            hid[:, h * HALF : (h + 1) * HALF], gs[:, cols], TN, preferred_element_type=F32
-        )
-
-    def partner_grads():
+    def gate_up_grads():
+        for k in range(3):
+            weight_copy(k).wait_send()
+
         def tile(j, carry):
-            rows, both = gate_up_tile(j, 1)
-            gu_send[0, rows, :] = both[:, :HALF].astype(BF16)
-            gu_send[1, rows, :] = both[:, HALF:].astype(BF16)
+            rows = pl.ds(pl.multiple_of(j * 256, 256), 256)
+            both = lax.dot_general(xs[:, rows], giui[...], TN, preferred_element_type=F32)
+            wgu[rows, :] = both.astype(BF16)
             return carry
 
         lax.fori_loop(0, 8, tile, 0)
         grad_copy(0).start()
         grad_copy(1).start()
 
+    def down_grads():
         def tile_down(j, carry):
-            cols, part = down_tile(j, 1)
-            d_send[:, cols] = part.astype(BF16)
+            cols = pl.ds(pl.multiple_of(j * 512, 512), 512)
+            both = lax.dot_general(hid[...], gs[:, cols], TN, preferred_element_type=F32)
+            wd[:, cols] = both.astype(BF16)
             return carry
 
         lax.fori_loop(0, 4, tile_down, 0)
@@ -462,24 +459,24 @@
         )[k]
         return pltpu.make_async_copy(src, dst, store_sem.at[k])
 
-    def own_grads():
-        grad_copy(0).wait_recv()
-        grad_copy(1).wait_recv()
-
-        def tile(j, carry):
-            rows, both = gate_up_tile(j, 0)
-            gu_recv[0, rows, :] = (both[:, :HALF] + gu_recv[0, rows, :].astype(F32)).astype(BF16)
-            gu_recv[1, rows, :] = (both[:, HALF:] + gu_recv[1, rows, :].astype(F32)).astype(BF16)
-            return carry
-
-        lax.fori_loop(0, 8, tile, 0)
-        store(0).start()
-        store(1).start()
+    def add_grads():
+        for k in range(2):
+            grad_copy(k).wait_recv()
+
+            def tile(j, carry):
+                rows = pl.ds(pl.multiple_of(j * 256, 256), 256)
+                total = wgu[rows, k * HALF : (k + 1) * HALF].astype(F32) + gu_recv[k, rows, :].astype(F32)
+                gu_recv[k, rows, :] = total.astype(BF16)
+                return carry
+
+            lax.fori_loop(0, 8, tile, 0)
+            store(k).start()
         grad_copy(2).wait_recv()
 
         def tile_down(j, carry):
-            cols, part = down_tile(j, 0)
-            d_recv[:, cols] = (part + d_recv[:, cols].astype(F32)).astype(BF16)
+            cols = pl.ds(pl.multiple_of(j * 512, 512), 512)
+            total = wd[0:HALF, cols].astype(F32) + d_recv[:, cols].astype(F32)
+            d_recv[:, cols] = total.astype(BF16)
             return carry
 
         lax.fori_loop(0, 4, tile_down, 0)
@@ -512,12 +509,13 @@
     send_back(1)
     send_back(0)
     send_back(3)
-    partner_grads()
+    gate_up_grads()
     combine_single(1)
     combine(2)
+    down_grads()
     combine(1)
     combine(0)
-    own_grads()
+    add_grads()
     combine_single(0)
     for block in (0, 2, 1, 3):
         cols = pl.ds(block * 512, 512)
@@ -532,7 +530,6 @@
             for piece in pieces(direction, h):
                 hop(direction, h, piece).wait_send()
     for k in range(3):
-        weight_copy(k).wait_send()
         grad_copy(k).wait_send()
     for h in range(1, 5):
         for block in range(4):
@@ -600,8 +597,6 @@
             pltpu.VMEM((ROWS, D), BF16),
             pltpu.VMEM((ROWS, D), F32),
             pltpu.VMEM((2, D, HALF), BF16),
-            pltpu.VMEM((2, D, HALF), BF16),
-            pltpu.VMEM((HALF, D), BF16),
             pltpu.VMEM((HALF, D), BF16),
             dma((7,)),
             dma((4,)),

time: 105 us -> 103 us (0.981)
  Pallas kernels: 104 us -> 102 us
    pallas_call x1, Pallas kernels: 101 us -> 99.8 us  [per_device(): pl.pallas_call(kernel, out_shape=(jax.ShapeDtypeStruct((ROWS, D), BF16),...]
where the time goes in v4:
time: 103 us
  Pallas kernels  102 us (99%)
    pallas_call x1, Pallas kernels, per_device(): pl.pallas_call(kernel, out_shape=(jax.ShapeDtypeStruct((ROWS, D), BF16),...  99.8 us
    pallas_call x1, Pallas kernels, per_device(): pl.pallas_call(store_out, out_shape=tuple((jax.ShapeDtypeStruct(x.shape,...  2.28 us

profile of v4, /device:TPU:8, one launch (start us, length us, event | category | flops | bytes accessed | tf_op | source)
XLA Modules:
  0.0 102.7 jit_solution(7105738610184468382)
XLA Ops:
  0.6 99.8 %shard_map.102 = (bf16[48,2048]{1,0:T(8,128)(2,1)S(1)}, bf16[2048,384]{1,0:T(8,128)(2,1)S(1)}, bf16[2048,384]{1,0:T(8,128)(2,1)S(1)}, bf16[384,2048]{1,0:T(8,128)(2,1)S(1)}) custom-call(bf16[48,2048]{1,0:T(8,128)(2,1)} %tok_hbm.1, bf16[48,2048]{1,0:T(8,128)(2,1)} %grad_hbm.1, s32[8,48]{1,0:T(8,128)} %bitcast.11, f32[8,48]{1,0:T(8,128)} %bitcast.12, ...), custom_call_target="tpu_custom_call" | custom-call | tf_op jit(solution)/shard_map/pallas_call | solution.py:563
  100.4 2.3 %shard_map.103 = (bf16[48,2048]{1,0:T(8,128)(2,1)}, bf16[2048,384]{1,0:T(8,128)(2,1)}, bf16[2048,384]{1,0:T(8,128)(2,1)}, bf16[384,2048]{1,0:T(8,128)(2,1)}) custom-call(bf16[48,2048]{1,0:T(8,128)(2,1)S(1)} %get-tuple-element.12.refs_0_, bf16[2048,384]{1,0:T(8,128)(2,1)S(1)} %get-tuple-element.13.refs_1_, bf16[2048,384]{1,0:T(8,128)(2,1)S(1)} %get-tuple-element.14.refs_2_, ...), custom_call_target="tpu_custom_call" | custom-call | tf_op jit(solution)/shard_map/pallas_call | solution.py:626

commit v5 on v4

--- a/solution.py
+++ b/solution.py
@@ -40,7 +40,8 @@
     partner = (z, p * 2 + 1 - core)
 
     def plane(i):
-        return ((py + i // 4) % 4) * 4 + (px + i % 4) % 4
+        k = (i * 7) % 16
+        return ((py + k // 4) % 4) * 4 + (px + k % 4) % 4
 
     def zdev(d):
         return ((z + d) % REP, e)

time: 103 us -> 103 us (level); the launches traced: 103 us -> 102 us
    pallas_call x1, Pallas kernels: 99.8 us -> 98.7 us  [per_device(): pl.pallas_call(kernel, out_shape=(jax.ShapeDtypeStruct((ROWS, D), BF16),...]
where the time goes in v5:
time: 103 us; the launch traced here: 102 us
  Pallas kernels  101 us (98%)
    pallas_call x1, Pallas kernels, per_device(): pl.pallas_call(kernel, out_shape=(jax.ShapeDtypeStruct((ROWS, D), BF16),...  98.7 us
    pallas_call x1, Pallas kernels, per_device(): pl.pallas_call(store_out, out_shape=tuple((jax.ShapeDtypeStruct(x.shape,...  2.28 us

profile of v5, /device:TPU:8, one launch (start us, length us, event | category | flops | bytes accessed | tf_op | source)
XLA Modules:
  0.0 101.7 jit_solution(7346080105166822558)
XLA Ops:
  0.6 98.7 %shard_map.102 = (bf16[48,2048]{1,0:T(8,128)(2,1)S(1)}, bf16[2048,384]{1,0:T(8,128)(2,1)S(1)}, bf16[2048,384]{1,0:T(8,128)(2,1)S(1)}, bf16[384,2048]{1,0:T(8,128)(2,1)S(1)}) custom-call(bf16[48,2048]{1,0:T(8,128)(2,1)} %tok_hbm.1, bf16[48,2048]{1,0:T(8,128)(2,1)} %grad_hbm.1, s32[8,48]{1,0:T(8,128)} %bitcast.11, f32[8,48]{1,0:T(8,128)} %bitcast.12, ...), custom_call_target="tpu_custom_call" | custom-call | tf_op jit(solution)/shard_map/pallas_call | solution.py:564
  99.4 2.3 %shard_map.103 = (bf16[48,2048]{1,0:T(8,128)(2,1)}, bf16[2048,384]{1,0:T(8,128)(2,1)}, bf16[2048,384]{1,0:T(8,128)(2,1)}, bf16[384,2048]{1,0:T(8,128)(2,1)}) custom-call(bf16[48,2048]{1,0:T(8,128)(2,1)S(1)} %get-tuple-element.12.refs_0_, bf16[2048,384]{1,0:T(8,128)(2,1)S(1)} %get-tuple-element.13.refs_1_, bf16[2048,384]{1,0:T(8,128)(2,1)S(1)} %get-tuple-element.14.refs_2_, ...), custom_call_target="tpu_custom_call" | custom-call | tf_op jit(solution)/shard_map/pallas_call | solution.py:627

commit v6 on v4

--- a/solution.py
+++ b/solution.py
@@ -320,7 +320,7 @@
             giui[rows, wide] = jnp.concatenate([gate_in, up_in], axis=1)
             return carry
 
-        lax.fori_loop(0, 2, forward, 0)
+        lax.fori_loop(0, 2, forward, 0, unroll=True)
 
         if g == 3:
             def back_single(j, carry):
@@ -335,7 +335,7 @@
                     srsend[c, :, :, cols] = packed.astype(BF16)
                 return carry
 
-            lax.fori_loop(0, 2, back_single, 0)
+            lax.fori_loop(0, 2, back_single, 0, unroll=True)
             return
 
         def back(j, carry):
@@ -347,7 +347,7 @@
             rsend[g, :, :, out] = both.astype(BF16)
             return carry
 
-        lax.fori_loop(0, 2, back, 0)
+        lax.fori_loop(0, 2, back, 0, unroll=True)
 
     def send_back(g):
         def go(i, carry):

time: 103 us -> 102 us (level)
  no operation moved by 1% of the time
where the time goes in v6:
time: 102 us
  Pallas kernels  101 us (99%)
    pallas_call x1, Pallas kernels, per_device(): pl.pallas_call(kernel, out_shape=(jax.ShapeDtypeStruct((ROWS, D), BF16),...  98.9 us
    pallas_call x1, Pallas kernels, per_device(): pl.pallas_call(store_out, out_shape=tuple((jax.ShapeDtypeStruct(x.shape,...  2.28 us

profile of v6, /device:TPU:8, one launch (start us, length us, event | category | flops | bytes accessed | tf_op | source)
XLA Modules:
  0.0 101.9 jit_solution(15483336041999027819)
XLA Ops:
  0.6 98.9 %shard_map.102 = (bf16[48,2048]{1,0:T(8,128)(2,1)S(1)}, bf16[2048,384]{1,0:T(8,128)(2,1)S(1)}, bf16[2048,384]{1,0:T(8,128)(2,1)S(1)}, bf16[384,2048]{1,0:T(8,128)(2,1)S(1)}) custom-call(bf16[48,2048]{1,0:T(8,128)(2,1)} %tok_hbm.1, bf16[48,2048]{1,0:T(8,128)(2,1)} %grad_hbm.1, s32[8,48]{1,0:T(8,128)} %bitcast.11, f32[8,48]{1,0:T(8,128)} %bitcast.12, ...), custom_call_target="tpu_custom_call" | custom-call | tf_op jit(solution)/shard_map/pallas_call | solution.py:563
  99.5 2.3 %shard_map.103 = (bf16[48,2048]{1,0:T(8,128)(2,1)}, bf16[2048,384]{1,0:T(8,128)(2,1)}, bf16[2048,384]{1,0:T(8,128)(2,1)}, bf16[384,2048]{1,0:T(8,128)(2,1)}) custom-call(bf16[48,2048]{1,0:T(8,128)(2,1)S(1)} %get-tuple-element.12.refs_0_, bf16[2048,384]{1,0:T(8,128)(2,1)S(1)} %get-tuple-element.13.refs_1_, bf16[2048,384]{1,0:T(8,128)(2,1)S(1)} %get-tuple-element.14.refs_2_, ...), custom_call_target="tpu_custom_call" | custom-call | tf_op jit(solution)/shard_map/pallas_call | solution.py:626
